TPU v7x, 256 devices: a whole 4x4x8 slice. The times are simulated.
256 devices in a mesh: dp: 16 (over y, z_hi, core), grp: 16 (over x, z_lo).
Axes of the slice: x: 4, y: 4, z: 8 (z_hi: 2, z_lo: 4; z = z_hi * 4 + z_lo), core: 2. Of those that a mesh axis runs over, the one named last changes fastest.
Arguments:
- partial_grads: bfloat16 [16, 192, 512, 512], P('dp', None, 'grp'), may hold values from -6 to 6
- owners: int32 [16, 12, 1], P('dp'), may hold values from 0 to 15; in each aligned block of 12 rows (0 to 11, 12 to 23, ..., all dimensions but the last counted through in order) at most 2 rows name the same one
- prev_stats: float32 [16, 16, 2, 2, 512, 512], P('dp', 'grp'), may hold values from -8 to 61440, as said below
Outputs:
- directions: float32 [192, 512, 512], P('dp', 'grp')
Inputs may be any that keep to these rules, and one draw needn't show every extreme that they name: `owners`: among the 12 blocks of one dp index no owner appears more than 2 times. `prev_stats`: each slot holds two symmetric positive definite matrices.
All inputs are finite; a program needn't handle non-finite values.
Results may differ from a plain program's by a relative error of at most 0.0029.
Values may be sent and summed in bfloat16 or wider, within the bound.
No kernel may reach another device: no remote copies, remote signals or barrier semaphores. Data moves between devices by JAX's collectives and lax.ppermute only.
A program may use at most 128 MiB of HBM per device.

v0:
```python
import jax
import jax.numpy as jnp
from jax import lax
from jax.sharding import PartitionSpec as P

ITERS = 2


def matmul_high(left_side, right_side):
    return jnp.matmul(left_side, right_side, precision=lax.Precision.HIGHEST)


def inverse_root(stats):
    width = stats.shape[-1]
    identity = jnp.eye(width, dtype=jnp.float32)
    frobenius = width * jnp.sqrt(jnp.mean(stats * stats, axis=(-2, -1), keepdims=True) + 1e-06)
    matrix = (stats / frobenius + 0.1 * identity) / 1.1
    root = identity
    for step in range(ITERS):
        factor = (5.0 * identity - matrix) * 0.25
        if step == 0:
            root = factor * 1.1 ** (-0.25)
        else:
            root = matmul_high(root, factor)
        if step + 1 < ITERS:
            square = matmul_high(factor, factor)
            fourth = matmul_high(square, square)
            matrix = matmul_high(fourth, matrix)
    return root


def owned_directions(owned, stats):
    left_gram = jnp.einsum("kab,kcb->kac", owned, owned, preferred_element_type=jnp.float32)
    right_gram = jnp.einsum("kba,kbc->kac", owned, owned, preferred_element_type=jnp.float32)
    grams = jnp.stack([left_gram, right_gram], axis=1)
    roots = inverse_root(0.5 * stats + 0.5 * grams)
    wide = owned.astype(jnp.float32)
    precond = matmul_high(matmul_high(roots[:, 0], wide), roots[:, 1])
    grad_mean = jnp.mean(wide * wide, axis=(1, 2), keepdims=True)
    pre_mean = jnp.mean(precond * precond, axis=(1, 2), keepdims=True)
    return precond * (jnp.sqrt(grad_mean) / jnp.sqrt(pre_mean + 1e-06))


def body(partial_grads, owners, prev_stats):
    local = partial_grads[0]
    summed = lax.psum_scatter(local.astype(jnp.float32), "dp", scatter_dimension=0, tiled=True)
    grad_rows = summed.astype(jnp.bfloat16)
    count, rows, width = grad_rows.shape
    groups = lax.axis_size("grp")
    places = prev_stats.shape[2]
    owner_row = owners[0, :, 0]
    same = owner_row[:, None] == owner_row[None, :]
    before = jnp.arange(count)[None, :] < jnp.arange(count)[:, None]
    slot = jnp.sum(jnp.where(same & before, 1, 0), axis=1).astype(jnp.int32)
    whole = lax.all_gather(grad_rows, "grp", axis=1, tiled=True)
    mine = lax.axis_index("grp")
    pick = (owner_row[None, :] == mine) & (slot[None, :] == jnp.arange(places)[:, None])
    owned = jnp.einsum(
        "kj,jab->kab", pick.astype(jnp.bfloat16), whole, preferred_element_type=jnp.float32
    ).astype(jnp.bfloat16)
    result = owned_directions(owned, prev_stats[0, 0])
    pieces = result.reshape(places, groups, rows, width)
    back = lax.all_to_all(pieces, "grp", split_axis=1, concat_axis=1, tiled=True)
    flat = back.reshape(places * groups, rows, width)
    return flat[slot * groups + owner_row]


def solution(mesh):
    in_specs = (
        P("dp", None, "grp", None),
        P("dp", None, None),
        P("dp", "grp", None, None, None, None),
    )
    out_specs = P("dp", "grp", None)
    return jax.shard_map(body, mesh=mesh, in_specs=in_specs, out_specs=out_specs, check_vma=False)
```

profile of v0, /device:TPU:1, one launch (start us, length us, event | category | flops | bytes accessed | tf_op | source)
XLA Modules:
  0.0 452.7 jit_solution(9899813148884714742)
XLA Ops:
  6.5 9.2 %bitcast_convert_fusion = f32[192,32,512]{2,1,0:T(8,128)} fusion(bf16[1,192,32,512]{3,2,1,0:T(8,128)(2,1)} %param.3), kind=kLoop, calls=%fused_computation.3 | loop fusion | flops 3145728 | bytes 18874368 | tf_op jit(solution)/shard_map/convert_element_type | solution.py:46
  15.8 179.1 %reduce-scatter.2.cloned.1.call-done = f32[12,32,512]{2,1,0:T(8,128)} async-done(((f32[192,32,512]{2,1,0:T(8,128)}), f32[12,32,512]{2,1,0:T(8,128)}) %reduce-scatter.2.cloned.1.call-update) | async-done | bytes 786448 | tf_op jit(solution)/shard_map/reduce_scatter | solution.py:46
  194.9 1.9 convert_element_type.19
  196.8 0.2 select_reduce_fusion
  197.0 0.2 fusion.15
  197.3 140.5 %all-gather.2.cloned.1.call-done = bf16[12,512,512]{2,1,0:T(8,128)(2,1)} async-done(((bf16[12,32,512]{2,1,0:T(8,128)(2,1)}), bf16[12,512,512]{2,1,0:T(8,128)(2,1)}) %all-gather.2.cloned.1.call-update) | async-done | bytes 6291472 | tf_op jit(solution)/shard_map/all_gather | solution.py:55
  337.8 6.9 %multiply_reduce_fusion.2 = (f32[2]{0:T(128)S(1)}, bf16[2,512,512]{2,0,1:T(2,128)(2,1)S(1)}) fusion(bf16[12,512,512]{2,1,0:T(8,128)(2,1)} %all-gather.2.cloned.1.call-done, pred[12]{0:T(512)(128)(4,1)S(1)} %broadcast_compare_fusion, s32[12]{0:T(128)S(1)} %select_reduce_fusion), kind=kOutput, calls=%fused_computation.23 | convolution fusion | flops 14680110 | bytes 7340100 | tf_op jit(solution)/shard_map/kj,jab->kab/dot_general | solution.py:58
  344.7 0.8 convolution_bitcast_fusion
  345.4 0.8 convolution_bitcast_fusion.1
  346.2 0.7 copy-done
  346.9 1.0 multiply_reduce_fusion
  347.9 2.2 subtract_multiply_fusion.2
  350.1 7.7 %fusion.8 = f32[2,2,512,512]{3,2,1,0:T(8,128)S(1)} fusion(f32[2,2,512,512]{3,2,0,1:T(8,128)S(1)} %get-tuple-element.6, f32[512,512]{1,0:T(8,128)S(1)} %get-tuple-element.12), kind=kOutput, calls=%fused_computation.11 | convolution fusion | flops 6444548096 | bytes 9437184 | tf_op jit(solution)/shard_map/dot_general | solution.py:10
  357.8 7.6 %fusion.3 = f32[2,2,512,512]{3,2,0,1:T(8,128)S(1)} fusion(f32[2,2,512,512]{3,2,1,0:T(8,128)S(1)} %fusion.8), kind=kOutput, calls=%fused_computation.6 | convolution fusion | flops 6442450944 | bytes 8388608 | tf_op jit(solution)/shard_map/dot_general | solution.py:10
  365.4 7.5 %subtract_multiply_fusion = f32[2,2,512,512]{3,2,0,1:T(8,128)S(1)} fusion(f32[2,2,512,512]{3,2,0,1:T(8,128)S(1)} %fusion.3, f32[2,2,512,512]{3,2,0,1:T(8,128)S(1)} %get-tuple-element.6, f32[512,512]{1,0:T(8,128)S(1)} %get-tuple-element.12), kind=kOutput, calls=%fused_computation.13 | convolution fusion | flops 6444548096 | bytes 13631488 | tf_op jit(solution)/shard_map/dot_general | solution.py:10
  372.8 7.3 %fusion.5 = f32[2,2,512,512]{3,2,1,0:T(8,128)S(1)} fusion(f32[2,2,512,512]{3,2,0,1:T(8,128)S(1)} %subtract_multiply_fusion, f32[2,2,512,512]{3,2,0,1:T(8,128)S(1)} %get-tuple-element.5), kind=kOutput, calls=%fused_computation.8 | convolution fusion | flops 6442450944 | bytes 12582912 | tf_op jit(solution)/shard_map/dot_general | solution.py:10
  380.1 1.8 fusion.11
  381.9 3.8 multiply_reduce_fusion.1
  385.7 0.3 broadcast_multiply_fusion
  386.0 1.6 copy.46
  387.6 3.7 all-to-all-start
  391.3 49.7 %all-to-all-done = f32[2,16,32,512]{3,2,0,1:T(8,128)S(1)} async-done(((f32[2,16,32,512]{3,2,0,1:T(8,128)}), f32[2,16,32,512]{3,2,0,1:T(8,128)S(1)}, u32[]{:S(2)}, u32[]{:S(2)}) %all-to-all-start) | async-done | bytes 2097184 | tf_op jit(solution)/shard_map/all_to_all | solution.py:63
  441.0 1.6 copy.47
  442.6 3.1 gather_fusion
  (12 shorter events, 0.1 us)
Async XLA Ops:
  6.5 188.3 %reduce-scatter.2.cloned.1.call-start = ((), (), s32[]{:S(2)}) async-start(), calls=%async_computation.2 | async-start | bytes 13369344 | tf_op jit(solution)/shard_map/reduce_scatter | solution.py:46
  15.7 181.1 %copy-start.1 = (s32[1,12,1]{1,2,0:T(1,128)S(1)}, s32[1,12,1]{1,2,0:T(1,128)}, u32[]{:S(2)}) copy-start(s32[1,12,1]{1,2,0:T(1,128)} %param.4) | copy-start | bytes 148
  15.7 322.0 %all-gather.2.cloned.1.call-start = ((), (), s32[]{:S(2)}) async-start(), calls=%async_computation.3 | async-start | bytes 6684672 | tf_op jit(solution)/shard_map/all_gather | solution.py:55
  344.7 2.2 copy-start
  387.6 53.5 %all-to-all-start = ((f32[2,16,32,512]{3,2,0,1:T(8,128)}), f32[2,16,32,512]{3,2,0,1:T(8,128)S(1)}, u32[]{:S(2)}, u32[]{:S(2)}) async-start(f32[2,16,32,512]{3,2,0,1:T(8,128)} %copy.46), calls=%async_computation.1 | async-start | bytes 4194304 | tf_op jit(solution)/shard_map/all_to_all | solution.py:63
Sparse Core Ops, SparseCore 0:
  15.8 178.9 reduce-scatter.1
  196.9 140.7 all-gather.1
where the time goes:
time: 459 us; the launch traced here: 453 us
  waiting for transfers between devices  369 us (80%)
  matrix products  44 us (10%)
  other arithmetic  15.1 us (3%)
  between operations  13.8 us (3%)
  local copies, waits for them, and re-layouts  6.86 us (1%)
    reduce_scatter x1, waiting for transfers between devices, body(): lax.psum_scatter(local.astype(jnp.float32), 'dp', scatter_dimension=0, ti...  179 us
    all_gather x1, waiting for transfers between devices, body(): whole = lax.all_gather(grad_rows, 'grp', axis=1, tiled=True)  140 us
    all_to_all x1, waiting for transfers between devices, body(): lax.all_to_all(pieces, 'grp', split_axis=1, concat_axis=1, tiled=True)  49.7 us
    dot_general x6, matrix products, matmul_high(): return jnp.matmul(left_side, right_side, precision=lax.Precision.HIGHEST)  35.6 us
  transfers between devices with their start and end apart: 3, of which 3 were waited for; matrix products, arithmetic and copies ran while one was open for 0% of the time, Pallas kernels for 0%

commit v1 on v0

v1 whole, which is shorter than its diff:
```python
from math import comb

import jax
import jax.numpy as jnp
from jax import lax
from jax.experimental import pallas as pl
from jax.experimental.pallas import tpu as pltpu
from jax.sharding import PartitionSpec as P

NY, NZ, NC = 4, 2, 2
SCALE = 1024.0
MIB = 1024 * 1024


def dp_perm(dy=0, dz=0, dc=0):
    pairs = []
    for y in range(NY):
        for z in range(NZ):
            for c in range(NC):
                source = (y * NZ + z) * NC + c
                target = (((y + dy) % NY) * NZ + (z + dz) % NZ) * NC + (c + dc) % NC
                pairs.append((source, target))
    return pairs


CORE = dp_perm(dc=1)
ZHI = dp_perm(dz=1)
UP = dp_perm(dy=1)
DOWN = dp_perm(dy=-1)


def root_coefficients():
    f0, f1 = 27.0 / 22.0, -5.0 / 22.0
    fifth = [comb(5, i) * f0 ** (5 - i) * f1**i for i in range(6)]
    product = [0.0] * 7
    for i, value in enumerate(fifth):
        product[i] += value / 11.0
        product[i + 1] += value * 10.0 / 11.0
    coefs = [-value / 4.0 for value in product]
    coefs[0] += 5.0 * f0 / 4.0
    coefs[1] += 5.0 * f1 / 4.0
    return [value * 1.1 ** (-0.25) for value in coefs]


COEF = root_coefficients()


def dot(a, b, dims=((1,), (0,))):
    return lax.dot_general(a, b, (dims, ((), ())), preferred_element_type=jnp.float32)


def root_rest(stats):
    width = stats.shape[-1]
    mean = jnp.sum(stats * stats, axis=(0, 1), keepdims=True) * (1.0 / (width * width))
    b1 = stats * (1.0 / (width * jnp.sqrt(mean + 1e-06)))
    b1h = b1.astype(jnp.bfloat16)
    b2 = dot(b1h, b1h)
    b2h = b2.astype(jnp.bfloat16)
    b3 = dot(b2h, b1h)
    b3h = b3.astype(jnp.bfloat16)
    high = COEF[4] * b1 + COEF[5] * b2 + COEF[6] * b3
    rest = COEF[1] * b1 + COEF[2] * b2 + COEF[3] * b3 + dot(b3h, high.astype(jnp.bfloat16))
    return rest.astype(jnp.bfloat16)


def direction_kernel(pieces_ref, stats_ref, out_ref):
    groups, _, rows, width = pieces_ref.shape
    grad = pieces_ref[...].reshape(groups * rows, width)
    left = root_rest(0.5 * stats_ref[0, 0] + 0.5 * dot(grad, grad, ((1,), (1,))))
    right = root_rest(0.5 * stats_ref[0, 1] + 0.5 * dot(grad, grad, ((0,), (0,))))
    wide = grad.astype(jnp.float32)
    half = COEF[0] * wide + dot(left, grad)
    pre = COEF[0] * half + dot(half.astype(jnp.bfloat16), right)
    count = 1.0 / (groups * rows * width)
    grad_mean = jnp.sum(wide * wide, axis=(0, 1), keepdims=True) * count
    pre_mean = jnp.sum(pre * pre, axis=(0, 1), keepdims=True) * count
    result = pre * (jnp.sqrt(grad_mean) / jnp.sqrt(pre_mean + 1e-06))
    out_ref[...] = result.astype(jnp.bfloat16).reshape(groups, 1, rows, width)


def directions(pieces, stats):
    groups, places, rows, width = pieces.shape
    return pl.pallas_call(
        direction_kernel,
        grid=(places,),
        in_specs=[
            pl.BlockSpec((groups, 1, rows, width), lambda k: (0, k, 0, 0)),
            pl.BlockSpec((1, 2, width, width), lambda k: (k, 0, 0, 0)),
        ],
        out_specs=pl.BlockSpec((groups, 1, rows, width), lambda k: (0, k, 0, 0)),
        out_shape=jax.ShapeDtypeStruct(pieces.shape, jnp.bfloat16),
        compiler_params=pltpu.CompilerParams(vmem_limit_bytes=48 * MIB),
    )(pieces, stats)


def pick_kernel(index_ref, in_ref, out_ref):
    for place in range(out_ref.shape[0]):
        out_ref[place] = in_ref[index_ref[place]].astype(out_ref.dtype)


def pick(index, array, dtype):
    return pl.pallas_call(
        pick_kernel,
        in_specs=[
            pl.BlockSpec(memory_space=pltpu.SMEM),
            pl.BlockSpec(memory_space=pltpu.VMEM),
        ],
        out_specs=pl.BlockSpec(memory_space=pltpu.VMEM),
        out_shape=jax.ShapeDtypeStruct(index.shape + array.shape[1:], dtype),
        compiler_params=pltpu.CompilerParams(vmem_limit_bytes=16 * MIB),
    )(index, array)


def send(array, perm):
    return lax.ppermute(array, "dp", perm)


def wide(array):
    return array.astype(jnp.float32)


def coded(array):
    return array.astype(jnp.float16)


def summed_rows(local, count):
    me = lax.axis_index("dp")
    y, z, c = me // (NZ * NC), (me // NC) % NZ, me % NC
    half = count // 2

    def part(dy, dz, dc):
        block = (((y + dy) % NY) * NZ + (z + dz) % NZ) * NC + (c + dc) % NC
        return lax.dynamic_slice_in_dim(local, block * count, count, axis=0)

    def both_cores(dy, dz):
        other = send(part(dy, dz, 1), CORE)
        return (wide(part(dy, dz, 0)) + wide(other)) * SCALE

    def over_y(dz):
        far = both_cores(2, dz)
        up_far = send(coded(far[:half]), UP)
        down_far = send(coded(far[half:]), DOWN)
        above = both_cores(1, dz)
        below = both_cores(3, dz)
        from_below_late = send(coded(above[half:]), UP)
        from_above_early = send(coded(below[:half]), DOWN)
        from_below_early = send(coded(above[:half] + wide(up_far)), UP)
        from_above_late = send(coded(below[half:] + wide(down_far)), DOWN)
        mine = both_cores(0, dz)
        early = mine[:half] + (wide(from_below_early) + wide(from_above_early))
        late = mine[half:] + (wide(from_below_late) + wide(from_above_late))
        return early, late

    early, late = over_y(1)
    other = send(jnp.concatenate([coded(early), coded(late)]), ZHI)
    early, late = over_y(0)
    total = jnp.concatenate([early, late]) + wide(other)
    return (total * (1.0 / SCALE)).astype(jnp.bfloat16)


def body(partial_grads, owners, prev_stats):
    groups = lax.axis_size("grp")
    places = prev_stats.shape[2]
    owner_row = owners[0, :, 0]
    count = owner_row.shape[0]
    blocks = jnp.arange(count, dtype=jnp.int32)
    same = owner_row[:, None] == owner_row[None, :]
    before = blocks[None, :] < blocks[:, None]
    slot = jnp.sum(jnp.where(same & before, 1, 0), axis=1).astype(jnp.int32)
    place = owner_row * places + slot
    every = jnp.arange(groups * places, dtype=jnp.int32)
    held = jnp.sum(jnp.where(place[None, :] == every[:, None], blocks[None, :], 0), axis=1).astype(jnp.int32)

    grad_rows = summed_rows(partial_grads[0], count)
    _, rows, width = grad_rows.shape
    outgoing = pick(held, grad_rows, jnp.bfloat16).reshape(groups, places, rows, width)
    pieces = lax.all_to_all(outgoing, "grp", split_axis=0, concat_axis=0, tiled=True)
    result = directions(pieces, prev_stats[0, 0])
    back = lax.all_to_all(result, "grp", split_axis=0, concat_axis=0, tiled=True)
    return pick(place, back.reshape(groups * places, rows, width), jnp.float32)


def solution(mesh):
    in_specs = (
        P("dp", None, "grp", None),
        P("dp", None, None),
        P("dp", "grp", None, None, None, None),
    )
    out_specs = P("dp", "grp", None)
    return jax.shard_map(body, mesh=mesh, in_specs=in_specs, out_specs=out_specs, check_vma=False)
```

time: 459 us -> 136 us (0.30); the launches traced: 453 us -> 135 us
  waiting for transfers between devices: 369 us -> 19.2 us
  blocking collectives: 0 us -> 71.4 us
  matrix products: 44 us -> 0 us
  starting transfers between devices: 3.76 us -> 23.4 us
  between operations: 13.8 us -> 0.18 us
  Pallas kernels: 0 us -> 13.5 us
  other arithmetic: 15.1 us -> 4.53 us
    reduce_scatter x1 -> x0, waiting for transfers between devices: 179 us -> none  [body(): lax.psum_scatter(local.astype(jnp.float32), 'dp', scatter_dimension=0, ti...]
    all_gather x1 -> x0, waiting for transfers between devices: 140 us -> none  [body(): whole = lax.all_gather(grad_rows, 'grp', axis=1, tiled=True)]
    all_to_all x0 -> x2, blocking collectives: none -> 71.4 us  [the longest x1 41.5 us: body(): lax.all_to_all(outgoing, 'grp', split_axis=0, concat_axis=0, tiled=True)]
    all_to_all x1 -> x0, waiting for transfers between devices: 49.7 us -> none  [body(): lax.all_to_all(pieces, 'grp', split_axis=1, concat_axis=1, tiled=True)]
    dot_general x9 -> x0, matrix products: 44 us -> none  [the longest x6 35.6 us: matmul_high(): return jnp.matmul(left_side, right_side, precision=lax.Precision.HIGHEST)]
    ppermute x0 -> x21, starting transfers between devices: none -> 23.4 us  [send(): return lax.ppermute(array, 'dp', perm)]
    ppermute x0 -> x21, waiting for transfers between devices: none -> 19.2 us  [send(): return lax.ppermute(array, 'dp', perm)]
    pallas_call x0 -> x3, Pallas kernels: none -> 13.5 us  [the longest x1 11.4 us: directions(): pl.pallas_call(direction_kernel, grid=(places,), in_specs=[pl.BlockSpec((...]
  transfers between devices with their start and end apart: 3 -> 21, of which waited for: 3 -> 11; matrix products, arithmetic and copies ran while one was open for 0% -> 1% of each run, Pallas kernels for 0% -> 0%
where the time goes in v1:
time: 136 us; the launch traced here: 135 us
  blocking collectives  71.4 us (53%)
  starting transfers between devices  23.4 us (17%)
  waiting for transfers between devices  19.2 us (14%)
  Pallas kernels  13.5 us (10%)
  other arithmetic  4.53 us (3%)
  local copies, waits for them, and re-layouts  3.29 us (2%)
    all_to_all x1, blocking collectives, body(): lax.all_to_all(outgoing, 'grp', split_axis=0, concat_axis=0, tiled=True)  41.5 us
    all_to_all x1, blocking collectives, body(): lax.all_to_all(result, 'grp', split_axis=0, concat_axis=0, tiled=True)  30 us
    ppermute x21, starting transfers between devices, send(): return lax.ppermute(array, 'dp', perm)  23.4 us
    ppermute x21, waiting for transfers between devices, send(): return lax.ppermute(array, 'dp', perm)  19.2 us
    pallas_call x1, Pallas kernels, directions(): pl.pallas_call(direction_kernel, grid=(places,), in_specs=[pl.BlockSpec((...  11.4 us
    mul x1, other arithmetic, both_cores(): return (wide(part(dy, dz, 0)) + wide(other)) * SCALE  3.16 us
    dynamic_slice x1, local copies, waits for them, and re-layouts, part(): return lax.dynamic_slice_in_dim(local, block * count, count, axis=0)  3.15 us
  transfers between devices with their start and end apart: 21, of which 11 were waited for; matrix products, arithmetic and copies ran while one was open for 1% of the time, Pallas kernels for 0%

profile of v1, /device:TPU:1, one launch (start us, length us, event | category | flops | bytes accessed | tf_op | source)
XLA Modules:
  0.0 135.5 jit_solution(6831057138187574853)
XLA Ops:
  0.0 3.1 %dynamic-slice_bitcast_fusion.2 = (bf16[12,32,512]{2,1,0:T(8,128)(2,1)}, bf16[12,32,512]{2,1,0:T(8,128)(2,1)}, bf16[12,32,512]{2,1,0:T(8,128)(2,1)S(1)}, bf16[12...) fusion(bf16[1,192,32,512]{3,2,1,0:T(8,128)(2,1)} %param.3, ...), kind=kLoop, calls=%fused_computation.42 | loop fusion | bytes 6291488 | tf_op jit(solution)/shard_map/dynamic_slice | solution.py:133
  3.2 3.2 %collective-permute-start = (bf16[12,32,512]{2,1,0:T(8,128)(2,1)S(1)}, bf16[12,32,512]{2,1,0:T(8,128)(2,1)S(1)}, u32[]{:S(2)}, u32[]{:S(2)}) collective-permute-start(bf16[12,32,512]{2,1,0:T(8,128)(2,1)S(1)} %get-tuple-element.19), channel_id=1, source_target_pairs={{0,16},{16,0},{32,48},{48,32},{64,80},{80,64},{96,112},{112,96},{1... | collective-permute-start | bytes 1179656 | tf_op jit(solution)/shard_map/ppermute | solution.py:115
  6.4 0.5 collective-permute-start.10
  6.9 0.5 collective-permute-start.12
  8.1 0.8 collective-permute-done.1
  9.2 0.8 collective-permute-done.10
  10.8 0.6 collective-permute-done.2
  11.7 3.2 %fusion.5 = (f32[12,32,512]{2,1,0:T(8,128)S(1)}, f16[12,32,512]{2,1,0:T(8,128)(2,1)S(1)}, f32[12,32,512]{2,1,0:T(8,128)S(1)}, f32[12,32,512]{2,1,0:T(8,128)S(1)}...) fusion(bf16[12,32,512]{2,1,0:T(8,128)(2,1)S(1)} %collective-per, ...), kind=kLoop, calls=%fused_computation.9 | loop fusion | flops 6684672 | bytes 11796512 | tf_op jit(solution)/shard_map/mul | solution.py:137
  15.1 2.7 %collective-permute-start.18 = (f16[6,32,512]{2,1,0:T(8,128)(2,1)S(1)}, f16[6,32,512]{2,1,0:T(8,128)(2,1)S(1)}, u32[]{:S(2)}, u32[]{:S(2)}) collective-permute-start(f16[6,32,512]{2,1,0:T(8,128)(2,1)S(1)} %get-tuple-element.34), channel_id=1, source_target_pairs={{0,192},{16,208},{32,224},{48,240},{64,0},{80,16},{96,32},{112,48}... | collective-permute-start | bytes 589832 | tf_op jit(solution)/shard_map/ppermute | solution.py:115
  17.9 2.7 %collective-permute-start.8 = (f16[6,32,512]{2,1,0:T(8,128)(2,1)S(1)}, f16[6,32,512]{2,1,0:T(8,128)(2,1)S(1)}, u32[]{:S(2)}, u32[]{:S(2)}) collective-permute-start(f16[6,32,512]{2,1,0:T(8,128)(2,1)S(1)} %get-tuple-element.36), channel_id=1, source_target_pairs={{0,192},{16,208},{32,224},{48,240},{64,0},{80,16},{96,32},{112,48}... | collective-permute-start | bytes 589832 | tf_op jit(solution)/shard_map/ppermute | solution.py:115
  20.5 1.8 %collective-permute-done.13 = f16[6,32,512]{2,1,0:T(8,128)(2,1)S(1)} collective-permute-done((f16[6,32,512]{2,1,0:T(8,128)(2,1)S(1)}, f16[6,32,512]{2,1,0:T(8,128)(2,1)S(1)}, u32[]{:S(2)}, u32[]{:S(2)}) %collective-permute-start.13) | collective-permute-done | bytes 196640 | tf_op jit(solution)/shard_map/ppermute | solution.py:115
  22.8 2.7 %collective-permute-start.16 = (f16[6,32,512]{2,1,0:T(8,128)(2,1)S(1)}, f16[6,32,512]{2,1,0:T(8,128)(2,1)S(1)}, u32[]{:S(2)}, u32[]{:S(2)}) collective-permute-start(f16[6,32,512]{2,1,0:T(8,128)(2,1)S(1)} %get-tuple-element.25), channel_id=1, source_target_pairs={{0,192},{16,208},{32,224},{48,240},{64,0},{80,16},{96,32},{112,48}... | collective-permute-start | bytes 589832 | tf_op jit(solution)/shard_map/ppermute | solution.py:115
  25.5 1.1 collective-permute-done.3
  27.0 1.2 collective-permute-start.4
  28.4 1.6 %collective-permute-done.14 = f16[6,32,512]{2,1,0:T(8,128)(2,1)S(1)} collective-permute-done((f16[6,32,512]{2,1,0:T(8,128)(2,1)S(1)}, f16[6,32,512]{2,1,0:T(8,128)(2,1)S(1)}, u32[]{:S(2)}, u32[]{:S(2)}) %collective-permute-start.14) | collective-permute-done | bytes 196640 | tf_op jit(solution)/shard_map/ppermute | solution.py:115
  30.0 4.2 %collective-permute-done.17 = f16[6,32,512]{2,1,0:T(8,128)(2,1)S(1)} collective-permute-done((f16[6,32,512]{2,1,0:T(8,128)(2,1)S(1)}, f16[6,32,512]{2,1,0:T(8,128)(2,1)S(1)}, u32[]{:S(2)}, u32[]{:S(2)}) %collective-permute-start.17) | collective-permute-done | bytes 196640 | tf_op jit(solution)/shard_map/ppermute | solution.py:115
  34.2 0.6 collective-permute-start.6
  35.6 7.0 %collective-permute-start.20 = (f16[12,32,512]{2,1,0:T(8,128)(2,1)S(1)}, f16[12,32,512]{2,1,0:T(8,128)(2,1)S(1)}, u32[]{:S(2)}, u32[]{:S(2)}) collective-permute-start(f16[12,32,512]{2,1,0:T(8,128)(2,1)S(1)} %pad_maximum_fusion), channel_id=1, source_target_pairs={{0,32},{16,48},{32,0},{48,16},{64,96},{80,112},{96,64},{112,80},{1... | collective-permute-start | bytes 1179656 | tf_op jit(solution)/shard_map/ppermute | solution.py:115
  42.9 7.5 %collective-permute-done.20 = f16[12,32,512]{2,1,0:T(8,128)(2,1)S(1)} collective-permute-done((f16[12,32,512]{2,1,0:T(8,128)(2,1)S(1)}, f16[12,32,512]{2,1,0:T(8,128)(2,1)S(1)}, u32[]{:S(2)}, u32[]{:S(2)}) %collective-permute-start.20) | collective-permute-done | bytes 393248 | tf_op jit(solution)/shard_map/ppermute | solution.py:115
  50.6 0.6 shard_map.37
  51.2 41.5 %all_to_all.10.pieces_ref = bf16[16,2,32,512]{3,2,1,0:T(8,128)(2,1)S(1)} all-to-all(bf16[16,2,32,512]{3,2,1,0:T(8,128)(2,1)S(1)} %bitcast.45), channel_id=1, replica_groups=mesh['dp'=16,'grp'=16] {'grp'}, dimensions={0} | all-to-all | bytes 2097152 | tf_op jit(solution)/shard_map/all_to_all | solution.py:177
  92.7 11.4 %shard_map.38 = bf16[16,2,32,512]{3,2,1,0:T(8,128)(2,1)S(1)} custom-call(bf16[16,2,32,512]{3,2,1,0:T(8,128)(2,1)S(1)} %all_to_all.10.pieces_ref, f32[2,2,512,512]{3,2,1,0:T(8,128)} %bitcast.47), custom_call_target="tpu_custom_call" | custom-call | tf_op jit(solution)/shard_map/pallas_call | solution.py:83
  104.1 30.0 %all_to_all.11 = bf16[16,2,32,512]{3,2,1,0:T(8,128)(2,1)S(1)} all-to-all(bf16[16,2,32,512]{3,2,1,0:T(8,128)(2,1)S(1)} %shard_map.38), channel_id=1, replica_groups=mesh['dp'=16,'grp'=16] {'grp'}, dimensions={0} | all-to-all | bytes 2097152 | tf_op jit(solution)/shard_map/all_to_all | solution.py:179
  134.0 1.5 %shard_map.39 = f32[12,32,512]{2,1,0:T(8,128)} custom-call(s32[12]{0:T(128)S(1)} %multiply_add_fusion.index_ref, bf16[32,32,512]{2,1,0:T(8,128)(2,1)S(1)} %bitcast.46), custom_call_target="tpu_custom_call" | custom-call | tf_op jit(solution)/shard_map/pallas_call | solution.py:102
  (40 shorter events, 4.7 us)
Async XLA Ops:
  0.0 10.4 %copy-start = (s32[1,12,1]{1,2,0:T(1,128)S(1)}, s32[1,12,1]{1,2,0:T(1,128)}, u32[]{:S(2)}) copy-start(s32[1,12,1]{1,2,0:T(1,128)} %param.4) | copy-start | bytes 148
  3.2 4.6 %collective-permute-start = (bf16[12,32,512]{2,1,0:T(8,128)(2,1)S(1)}, bf16[12,32,512]{2,1,0:T(8,128)(2,1)S(1)}, u32[]{:S(2)}, u32[]{:S(2)}) collective-permute-start(bf16[12,32,512]{2,1,0:T(8,128)(2,1)S(1)} %get-tuple-element.19), channel_id=1, source_target_pairs={{0,16},{16,0},{32,48},{48,32},{64,80},{80,64},{96,112},{112,96},{1... | collective-permute-start | bytes 1179656 | tf_op jit(solution)/shard_map/ppermute | solution.py:115
  6.4 2.5 %collective-permute-start.1 = (bf16[12,32,512]{2,1,0:T(8,128)(2,1)S(1)}, bf16[12,32,512]{2,1,0:T(8,128)(2,1)S(1)}, u32[]{:S(2)}, u32[]{:S(2)}) collective-permute-start(bf16[12,32,512]{2,1,0:T(8,128)(2,1)S(1)} %get-tuple-element.18), channel_id=1, source_target_pairs={{0,16},{16,0},{32,48},{48,32},{64,80},{80,64},{96,112},{112,96},{1... | collective-permute-start | bytes 1179656 | tf_op jit(solution)/shard_map/ppermute | solution.py:115
  6.4 3.6 %collective-permute-start.10 = (bf16[12,32,512]{2,1,0:T(8,128)(2,1)S(1)}, bf16[12,32,512]{2,1,0:T(8,128)(2,1)S(1)}, u32[]{:S(2)}, u32[]{:S(2)}) collective-permute-start(bf16[12,32,512]{2,1,0:T(8,128)(2,1)S(1)} %get-tuple-element.15), channel_id=1, source_target_pairs={{0,16},{16,0},{32,48},{48,32},{64,80},{80,64},{96,112},{112,96},{1... | collective-permute-start | bytes 1179656 | tf_op jit(solution)/shard_map/ppermute | solution.py:115
  6.9 3.6 %collective-permute-start.11 = (bf16[12,32,512]{2,1,0:T(8,128)(2,1)}, bf16[12,32,512]{2,1,0:T(8,128)(2,1)S(1)}, u32[]{:S(2)}, u32[]{:S(2)}) collective-permute-start(bf16[12,32,512]{2,1,0:T(8,128)(2,1)} %get-tuple-element.13), channel_id=1, source_target_pairs={{0,16},{16,0},{32,48},{48,32},{64,80},{80,64},{96,112},{112,96},{1... | collective-permute-start | bytes 1179656 | tf_op jit(solution)/shard_map/ppermute | solution.py:115
  6.9 3.6 %collective-permute-start.12 = (bf16[12,32,512]{2,1,0:T(8,128)(2,1)}, bf16[12,32,512]{2,1,0:T(8,128)(2,1)S(1)}, u32[]{:S(2)}, u32[]{:S(2)}) collective-permute-start(bf16[12,32,512]{2,1,0:T(8,128)(2,1)} %get-tuple-element.14), channel_id=1, source_target_pairs={{0,16},{16,0},{32,48},{48,32},{64,80},{80,64},{96,112},{112,96},{1... | collective-permute-start | bytes 1179656 | tf_op jit(solution)/shard_map/ppermute | solution.py:115
  7.7 3.0 %collective-permute-start.15 = (bf16[12,32,512]{2,1,0:T(8,128)(2,1)}, bf16[12,32,512]{2,1,0:T(8,128)(2,1)S(1)}, u32[]{:S(2)}, u32[]{:S(2)}) collective-permute-start(bf16[12,32,512]{2,1,0:T(8,128)(2,1)} %get-tuple-element.20), channel_id=1, source_target_pairs={{0,16},{16,0},{32,48},{48,32},{64,80},{80,64},{96,112},{112,96},{1... | collective-permute-start | bytes 1179656 | tf_op jit(solution)/shard_map/ppermute | solution.py:115
  8.9 2.5 %collective-permute-start.2 = (bf16[12,32,512]{2,1,0:T(8,128)(2,1)}, bf16[12,32,512]{2,1,0:T(8,128)(2,1)S(1)}, u32[]{:S(2)}, u32[]{:S(2)}) collective-permute-start(bf16[12,32,512]{2,1,0:T(8,128)(2,1)} %get-tuple-element.17), channel_id=1, source_target_pairs={{0,16},{16,0},{32,48},{48,32},{64,80},{80,64},{96,112},{112,96},{1... | collective-permute-start | bytes 1179656 | tf_op jit(solution)/shard_map/ppermute | solution.py:115
  10.0 1.7 %collective-permute-start.5 = (bf16[12,32,512]{2,1,0:T(8,128)(2,1)S(1)}, bf16[12,32,512]{2,1,0:T(8,128)(2,1)S(1)}, u32[]{:S(2)}, u32[]{:S(2)}) collective-permute-start(bf16[12,32,512]{2,1,0:T(8,128)(2,1)S(1)} %get-tuple-element.16), channel_id=1, source_target_pairs={{0,16},{16,0},{32,48},{48,32},{64,80},{80,64},{96,112},{112,96},{1... | collective-permute-start | bytes 1179656 | tf_op jit(solution)/shard_map/ppermute | solution.py:115
  15.0 7.4 %collective-permute-start.13 = (f16[6,32,512]{2,1,0:T(8,128)(2,1)S(1)}, f16[6,32,512]{2,1,0:T(8,128)(2,1)S(1)}, u32[]{:S(2)}, u32[]{:S(2)}) collective-permute-start(f16[6,32,512]{2,1,0:T(8,128)(2,1)S(1)} %get-tuple-element.33), channel_id=1, source_target_pairs={{0,64},{16,80},{32,96},{48,112},{64,128},{80,144},{96,160},{112,17... | collective-permute-start | bytes 589832 | tf_op jit(solution)/shard_map/ppermute | solution.py:115
  15.1 7.6 %collective-permute-start.18 = (f16[6,32,512]{2,1,0:T(8,128)(2,1)S(1)}, f16[6,32,512]{2,1,0:T(8,128)(2,1)S(1)}, u32[]{:S(2)}, u32[]{:S(2)}) collective-permute-start(f16[6,32,512]{2,1,0:T(8,128)(2,1)S(1)} %get-tuple-element.34), channel_id=1, source_target_pairs={{0,192},{16,208},{32,224},{48,240},{64,0},{80,16},{96,32},{112,48}... | collective-permute-start | bytes 589832 | tf_op jit(solution)/shard_map/ppermute | solution.py:115
  17.8 8.8 %collective-permute-start.3 = (f16[6,32,512]{2,1,0:T(8,128)(2,1)S(1)}, f16[6,32,512]{2,1,0:T(8,128)(2,1)S(1)}, u32[]{:S(2)}, u32[]{:S(2)}) collective-permute-start(f16[6,32,512]{2,1,0:T(8,128)(2,1)S(1)} %get-tuple-element.35), channel_id=1, source_target_pairs={{0,64},{16,80},{32,96},{48,112},{64,128},{80,144},{96,160},{112,17... | collective-permute-start | bytes 589832 | tf_op jit(solution)/shard_map/ppermute | solution.py:115
  17.9 9.1 %collective-permute-start.8 = (f16[6,32,512]{2,1,0:T(8,128)(2,1)S(1)}, f16[6,32,512]{2,1,0:T(8,128)(2,1)S(1)}, u32[]{:S(2)}, u32[]{:S(2)}) collective-permute-start(f16[6,32,512]{2,1,0:T(8,128)(2,1)S(1)} %get-tuple-element.36), channel_id=1, source_target_pairs={{0,192},{16,208},{32,224},{48,240},{64,0},{80,16},{96,32},{112,48}... | collective-permute-start | bytes 589832 | tf_op jit(solution)/shard_map/ppermute | solution.py:115
  22.5 7.5 %collective-permute-start.14 = (f16[6,32,512]{2,1,0:T(8,128)(2,1)S(1)}, f16[6,32,512]{2,1,0:T(8,128)(2,1)S(1)}, u32[]{:S(2)}, u32[]{:S(2)}) collective-permute-start(f16[6,32,512]{2,1,0:T(8,128)(2,1)S(1)} %get-tuple-element.23), channel_id=1, source_target_pairs={{0,64},{16,80},{32,96},{48,112},{64,128},{80,144},{96,160},{112,17... | collective-permute-start | bytes 589832 | tf_op jit(solution)/shard_map/ppermute | solution.py:115
  22.6 11.6 %collective-permute-start.17 = (f16[6,32,512]{2,1,0:T(8,128)(2,1)S(1)}, f16[6,32,512]{2,1,0:T(8,128)(2,1)S(1)}, u32[]{:S(2)}, u32[]{:S(2)}) collective-permute-start(f16[6,32,512]{2,1,0:T(8,128)(2,1)S(1)} %get-tuple-element.24), channel_id=1, source_target_pairs={{0,64},{16,80},{32,96},{48,112},{64,128},{80,144},{96,160},{112,17... | collective-permute-start | bytes 589832 | tf_op jit(solution)/shard_map/ppermute | solution.py:115
  22.8 12.0 %collective-permute-start.16 = (f16[6,32,512]{2,1,0:T(8,128)(2,1)S(1)}, f16[6,32,512]{2,1,0:T(8,128)(2,1)S(1)}, u32[]{:S(2)}, u32[]{:S(2)}) collective-permute-start(f16[6,32,512]{2,1,0:T(8,128)(2,1)S(1)} %get-tuple-element.25), channel_id=1, source_target_pairs={{0,192},{16,208},{32,224},{48,240},{64,0},{80,16},{96,32},{112,48}... | collective-permute-start | bytes 589832 | tf_op jit(solution)/shard_map/ppermute | solution.py:115
  26.6 8.7 %collective-permute-start.19 = (f16[6,32,512]{2,1,0:T(8,128)(2,1)S(1)}, f16[6,32,512]{2,1,0:T(8,128)(2,1)S(1)}, u32[]{:S(2)}, u32[]{:S(2)}) collective-permute-start(f16[6,32,512]{2,1,0:T(8,128)(2,1)S(1)} %get-tuple-element.26), channel_id=1, source_target_pairs={{0,192},{16,208},{32,224},{48,240},{64,0},{80,16},{96,32},{112,48}... | collective-permute-start | bytes 589832 | tf_op jit(solution)/shard_map/ppermute | solution.py:115
  27.0 15.7 %collective-permute-start.4 = (f16[6,32,512]{2,1,0:T(8,128)(2,1)S(1)}, f16[6,32,512]{2,1,0:T(8,128)(2,1)S(1)}, u32[]{:S(2)}, u32[]{:S(2)}) collective-permute-start(f16[6,32,512]{2,1,0:T(8,128)(2,1)S(1)} %get-tuple-element.29), channel_id=1, source_target_pairs={{0,64},{16,80},{32,96},{48,112},{64,128},{80,144},{96,160},{112,17... | collective-permute-start | bytes 589832 | tf_op jit(solution)/shard_map/ppermute | solution.py:115
  30.0 12.7 %collective-permute-start.7 = (f16[6,32,512]{2,1,0:T(8,128)(2,1)S(1)}, f16[6,32,512]{2,1,0:T(8,128)(2,1)S(1)}, u32[]{:S(2)}, u32[]{:S(2)}) collective-permute-start(f16[6,32,512]{2,1,0:T(8,128)(2,1)S(1)} %get-tuple-element.30), channel_id=1, source_target_pairs={{0,64},{16,80},{32,96},{48,112},{64,128},{80,144},{96,160},{112,17... | collective-permute-start | bytes 589832 | tf_op jit(solution)/shard_map/ppermute | solution.py:115
  34.2 8.5 %collective-permute-start.6 = (f16[6,32,512]{2,1,0:T(8,128)(2,1)S(1)}, f16[6,32,512]{2,1,0:T(8,128)(2,1)S(1)}, u32[]{:S(2)}, u32[]{:S(2)}) collective-permute-start(f16[6,32,512]{2,1,0:T(8,128)(2,1)S(1)} %get-tuple-element.31), channel_id=1, source_target_pairs={{0,192},{16,208},{32,224},{48,240},{64,0},{80,16},{96,32},{112,48}... | collective-permute-start | bytes 589832 | tf_op jit(solution)/shard_map/ppermute | solution.py:115
  34.8 7.9 %collective-permute-start.9 = (f16[6,32,512]{2,1,0:T(8,128)(2,1)S(1)}, f16[6,32,512]{2,1,0:T(8,128)(2,1)S(1)}, u32[]{:S(2)}, u32[]{:S(2)}) collective-permute-start(f16[6,32,512]{2,1,0:T(8,128)(2,1)S(1)} %get-tuple-element.32), channel_id=1, source_target_pairs={{0,192},{16,208},{32,224},{48,240},{64,0},{80,16},{96,32},{112,48}... | collective-permute-start | bytes 589832 | tf_op jit(solution)/shard_map/ppermute | solution.py:115
  35.6 14.8 %collective-permute-start.20 = (f16[12,32,512]{2,1,0:T(8,128)(2,1)S(1)}, f16[12,32,512]{2,1,0:T(8,128)(2,1)S(1)}, u32[]{:S(2)}, u32[]{:S(2)}) collective-permute-start(f16[12,32,512]{2,1,0:T(8,128)(2,1)S(1)} %pad_maximum_fusion), channel_id=1, source_target_pairs={{0,32},{16,48},{32,0},{48,16},{64,96},{80,112},{96,64},{112,80},{1... | collective-permute-start | bytes 1179656 | tf_op jit(solution)/shard_map/ppermute | solution.py:115

commit v2 on v1

v2 whole, which is shorter than its diff:
```python
from math import comb

import jax
import jax.numpy as jnp
from jax import lax
from jax.experimental import pallas as pl
from jax.experimental.pallas import tpu as pltpu
from jax.sharding import PartitionSpec as P

NY, NZ, NC = 4, 2, 2
SCALE = 1024.0
MIB = 1024 * 1024


def dp_perm(target):
    pairs = []
    for y in range(NY):
        for z in range(NZ):
            for c in range(NC):
                ty, tz, tc = target(y, z, c)
                pairs.append(((y * NZ + z) * NC + c, (ty * NZ + tz) * NC + tc))
    return pairs


CORE = dp_perm(lambda y, z, c: (y, z, 1 - c))
NEXT = dp_perm(lambda y, z, c: (y ^ 1 if c == 0 else 3 - y, z, c))
LAST = dp_perm(lambda y, z, c: (3 - y if c == 0 else y ^ 1, z, c))
OTHER_Z = dp_perm(lambda y, z, c: (y, 1 - z, c))
OPPOSITE = dp_perm(lambda y, z, c: (y ^ 2, z, c))
NX, NLO = 4, 4


def ring_perm():
    pairs = []
    for dp in range(NY * NZ * NC):
        for grp in range(NX * NLO):
            y, hi, c = dp // (NZ * NC), (dp // NC) % NZ, dp % NC
            x, lo = grp // NLO, grp % NLO
            ring = (hi * NLO + lo + (2 if c == 0 else -2)) % (NZ * NLO)
            target = (y * NZ + ring // NLO) * NC + c
            pairs.append((dp * NX * NLO + grp, target * NX * NLO + x * NLO + ring % NLO))
    return pairs


ALONG_Z = ring_perm()


def root_coefficients():
    f0, f1 = 27.0 / 22.0, -5.0 / 22.0
    fifth = [comb(5, i) * f0 ** (5 - i) * f1**i for i in range(6)]
    product = [0.0] * 7
    for i, value in enumerate(fifth):
        product[i] += value / 11.0
        product[i + 1] += value * 10.0 / 11.0
    coefs = [-value / 4.0 for value in product]
    coefs[0] += 5.0 * f0 / 4.0
    coefs[1] += 5.0 * f1 / 4.0
    return [value * 1.1 ** (-0.25) for value in coefs]


COEF = root_coefficients()


def dot(a, b, dims=((1,), (0,))):
    return lax.dot_general(a, b, (dims, ((), ())), preferred_element_type=jnp.float32)


def gram_kernel(pieces_ref, stats_ref, out_ref, held, arrived):
    groups, places, rows, width = pieces_ref.shape
    size = groups * rows
    slots = range(places)
    chains = [(k, side) for k in slots for side in range(2)]
    copies = [pltpu.make_async_copy(stats_ref.at[k], held.at[k], arrived.at[k]) for k in slots]
    for copy in copies:
        copy.start()
    grads = [pieces_ref[:, k].reshape(size, width) for k in slots]
    grams = [dot(grads[k], grads[k], ((1 - side,), (1 - side,))) for k, side in chains]
    for copy in copies:
        copy.wait()
    sums = [held[k, side] + gram for (k, side), gram in zip(chains, grams)]
    scales = []
    for s in sums:
        mean = jnp.sum(s * s, axis=(0, 1), keepdims=True) * (0.25 / (width * width))
        scales.append(0.5 / (width * jnp.sqrt(mean + 1e-06)))
    b1 = [s * scale for s, scale in zip(sums, scales)]
    b1h = [b.astype(jnp.bfloat16) for b in b1]
    b2 = [dot(b, b) for b in b1h]
    b2h = [b.astype(jnp.bfloat16) for b in b2]
    b3 = [dot(p, q) for p, q in zip(b2h, b1h)]
    b3h = [b.astype(jnp.bfloat16) for b in b3]
    high = [(COEF[4] * p + COEF[5] * q + COEF[6] * r).astype(jnp.bfloat16) for p, q, r in zip(b1, b2, b3)]
    low = [COEF[1] * p + COEF[2] * q + COEF[3] * r for p, q, r in zip(b1, b2, b3)]
    rest = [(l + dot(p, q)).astype(jnp.bfloat16) for l, p, q in zip(low, b3h, high)]
    count = 1.0 / (size * width)
    wides = [grad.astype(jnp.float32) for grad in grads]
    halves = [COEF[0] * wides[k] + dot(rest[2 * k], grads[k]) for k in slots]
    pres = [COEF[0] * halves[k] + dot(halves[k].astype(jnp.bfloat16), rest[2 * k + 1]) for k in slots]
    for k in slots:
        grad_mean = jnp.sum(wides[k] * wides[k], axis=(0, 1), keepdims=True) * count
        pre_mean = jnp.sum(pres[k] * pres[k], axis=(0, 1), keepdims=True) * count
        result = pres[k] * (jnp.sqrt(grad_mean) / jnp.sqrt(pre_mean + 1e-06))
        out_ref[:, k] = result.astype(jnp.bfloat16).reshape(groups, rows, width)


def directions(pieces, stats):
    return pl.pallas_call(
        gram_kernel,
        in_specs=[
            pl.BlockSpec(memory_space=pltpu.VMEM),
            pl.BlockSpec(memory_space=pl.ANY),
        ],
        out_specs=pl.BlockSpec(memory_space=pltpu.VMEM),
        out_shape=jax.ShapeDtypeStruct(pieces.shape, jnp.bfloat16),
        scratch_shapes=[
            pltpu.VMEM(stats.shape, jnp.float32),
            pltpu.SemaphoreType.DMA((stats.shape[0],)),
        ],
        compiler_params=pltpu.CompilerParams(vmem_limit_bytes=48 * MIB),
    )(pieces, stats)


def pick_kernel(index_ref, in_ref, out_ref):
    for place in range(out_ref.shape[0]):
        out_ref[place] = in_ref[index_ref[place]].astype(out_ref.dtype)


def pick(index, array, dtype):
    return pl.pallas_call(
        pick_kernel,
        in_specs=[
            pl.BlockSpec(memory_space=pltpu.SMEM),
            pl.BlockSpec(memory_space=pltpu.VMEM),
        ],
        out_specs=pl.BlockSpec(memory_space=pltpu.VMEM),
        out_shape=jax.ShapeDtypeStruct(index.shape + array.shape[1:], dtype),
        compiler_params=pltpu.CompilerParams(vmem_limit_bytes=16 * MIB),
    )(index, array)


def send(array, perm):
    return lax.ppermute(array, "dp", perm)


def wide(array):
    return array.astype(jnp.float32)


def coded(array):
    return array.astype(jnp.float16)


def after(value, *others):
    return lax.optimization_barrier((value,) + others)[0]


def summed_rows(local, count):
    me = lax.axis_index("dp")
    y, z, c = me // (NZ * NC), (me // NC) % NZ, me % NC
    following = jnp.where(c == 0, y ^ 1, 3 - y)
    preceding = jnp.where(c == 0, 3 - y, y ^ 1)
    opposite = y ^ 2
    _, rows, width = local.shape
    parts = local.reshape(NY, NZ, NC, count, rows, width)

    def held(source, dz, dc):
        at = (0, z ^ dz, c ^ dc, 0, 0, 0)
        return lax.dynamic_slice(source, at, (NY, 1, 1, count, rows, width)).reshape(NY, count, rows, width)

    def part(at_y, dz, other):
        at = (at_y, z ^ dz, c, 0, 0, 0)
        mine = lax.dynamic_slice(parts, at, (1, 1, 1, count, rows, width)).reshape(count, rows, width)
        theirs = lax.dynamic_slice(other, (at_y, 0, 0, 0), (1, count, rows, width)).reshape(count, rows, width)
        return (wide(mine) + wide(theirs)) * SCALE

    to_core1 = held(parts, 1, 1)
    other1 = send(to_core1, CORE)
    other0 = send(held(after(parts, to_core1), 0, 1), CORE)
    first1 = coded(part(opposite, 1, other1)), coded(part(following, 1, other1))
    far1, near1 = (send(value, NEXT) for value in first1)
    second1 = coded(part(preceding, 1, other1) + wide(far1))
    last1 = send(second1, LAST)
    other0 = after(other0, second1)
    direct = [coded(part(at, 0, other0)) for at in (opposite, following, preceding)]
    crossing = coded(part(y, 1, after(other1, *direct)) + (wide(near1) + wide(last1)))
    crossed = send(crossing, OTHER_Z)
    along0 = [send(value, pairs) for value, pairs in zip(direct, (OPPOSITE, NEXT, LAST))]
    other0 = after(other0, crossing, *direct)
    mine = part(y, 0, other0) + (wide(along0[0]) + wide(along0[1]) + wide(along0[2]))
    whole = lax.optimization_barrier(mine)
    return ((whole + wide(crossed)) * (1.0 / SCALE)).astype(jnp.bfloat16)


def body(partial_grads, owners, prev_stats):
    groups = lax.axis_size("grp")
    places = prev_stats.shape[2]
    owner_row = owners[0, :, 0]
    count = owner_row.shape[0]
    blocks = jnp.arange(count, dtype=jnp.int32)
    same = owner_row[:, None] == owner_row[None, :]
    before = blocks[None, :] < blocks[:, None]
    slot = jnp.sum(jnp.where(same & before, 1, 0), axis=1).astype(jnp.int32)
    place = owner_row * places + slot
    every = jnp.arange(groups * places, dtype=jnp.int32)
    held = jnp.sum(jnp.where(place[None, :] == every[:, None], blocks[None, :], 0), axis=1).astype(jnp.int32)

    grad_rows = summed_rows(partial_grads[0], count)
    _, rows, width = grad_rows.shape
    outgoing = pick(held, grad_rows, jnp.bfloat16).reshape(groups, places, rows, width)
    pieces = lax.all_to_all(outgoing, "grp", split_axis=0, concat_axis=0, tiled=True)
    result = directions(pieces, prev_stats[0, 0])
    back = lax.all_to_all(result, "grp", split_axis=0, concat_axis=0, tiled=True)
    return pick(place, back.reshape(groups * places, rows, width), jnp.float32)


def solution(mesh):
    in_specs = (
        P("dp", None, "grp", None),
        P("dp", None, None),
        P("dp", "grp", None, None, None, None),
    )
    out_specs = P("dp", "grp", None)
    return jax.shard_map(body, mesh=mesh, in_specs=in_specs, out_specs=out_specs, check_vma=False)
```

time: 136 us -> 121 us (0.89)
  blocking collectives: 71.4 us -> 61.6 us
  starting transfers between devices: 23.4 us -> 15.3 us
  other arithmetic: 4.53 us -> 8.9 us
  Pallas kernels: 13.5 us -> 12.1 us
    all_to_all x1, blocking collectives: 41.5 us -> 32.2 us  [body(): lax.all_to_all(outgoing, 'grp', split_axis=0, concat_axis=0, tiled=True)]
    ppermute x21 -> x9, starting transfers between devices: 23.4 us -> 15.3 us  [send(): return lax.ppermute(array, 'dp', perm)]
    convert_element_type x3 -> x4, other arithmetic: 0.43 us -> 7.16 us  [coded(): return array.astype(jnp.float16)]
    reshape x0 -> x2, local copies, waits for them, and re-layouts: none -> 4.26 us  [held(): lax.dynamic_slice(source, at, (NY, 1, 1, count, rows, width))]
    mul x1 -> x0, other arithmetic: 3.16 us -> none  [both_cores(): return (wide(part(dy, dz, 0)) + wide(other)) * SCALE]
    dynamic_slice x1 -> x0, local copies, waits for them, and re-layouts: 3.15 us -> none  [part(): return lax.dynamic_slice_in_dim(local, block * count, count, axis=0)]
    ppermute x21 -> x9, waiting for transfers between devices: 19.2 us -> 18.7 us  [send(): return lax.ppermute(array, 'dp', perm)]
  transfers between devices with their start and end apart: 21 -> 9, of which waited for: 11 -> 6; matrix products, arithmetic and copies ran while one was open for 1% -> 8% of each run, Pallas kernels for 0% -> 0%
where the time goes in v2:
time: 121 us
  blocking collectives  61.6 us (51%)
  waiting for transfers between devices  18.7 us (15%)
  starting transfers between devices  15.3 us (13%)
  Pallas kernels  12.1 us (10%)
  other arithmetic  8.9 us (7%)
  local copies, waits for them, and re-layouts  4.26 us (4%)
    all_to_all x1, blocking collectives, body(): lax.all_to_all(outgoing, 'grp', split_axis=0, concat_axis=0, tiled=True)  32.2 us
    all_to_all x1, blocking collectives, body(): lax.all_to_all(result, 'grp', split_axis=0, concat_axis=0, tiled=True)  29.4 us
    ppermute x9, waiting for transfers between devices, send(): return lax.ppermute(array, 'dp', perm)  18.7 us
    ppermute x9, starting transfers between devices, send(): return lax.ppermute(array, 'dp', perm)  15.3 us
    pallas_call x1, Pallas kernels, directions(): pl.pallas_call(gram_kernel, in_specs=[pl.BlockSpec(memory_space=pltpu.VME...  10.1 us
    convert_element_type x4, other arithmetic, coded(): return array.astype(jnp.float16)  7.16 us
    reshape x2, local copies, waits for them, and re-layouts, held(): lax.dynamic_slice(source, at, (NY, 1, 1, count, rows, width))  4.26 us
  transfers between devices with their start and end apart: 9, of which 6 were waited for; matrix products, arithmetic and copies ran while one was open for 8% of the time, Pallas kernels for 0%

profile of v2, /device:TPU:1, one launch (start us, length us, event | category | flops | bytes accessed | tf_op | source)
XLA Modules:
  0.0 121.1 jit_solution(10837819825106388338)
XLA Ops:
  0.0 2.7 %dynamic-slice_bitcast_fusion.1 = bf16[4,12,32,512]{3,2,1,0:T(8,128)(2,1)} fusion(bf16[4,2,2,12,32,512]{5,4,3,2,1,0:T(8,128)(2,1)} %bitcast.60, s32[]{:T(128)S(6)} %select_n.93, s32[]{:T(128)S(6)} %select_n.94), kind=kLoop, calls=%fused_computation.1 | loop fusion | bytes 3145736 | tf_op jit(solution)/shard_map/reshape | solution.py:167
  2.7 3.2 %collective-permute-start.1 = (bf16[4,12,32,512]{3,2,1,0:T(8,128)(2,1)}, bf16[4,12,32,512]{3,2,1,0:T(8,128)(2,1)}, u32[]{:S(2)}, u32[]{:S(2)}) collective-permute-start(bf16[4,12,32,512]{3,2,1,0:T(8,128)(2,1)} %dynamic-slice_bitcast_fusion.1), channel_id=1, source_target_pairs={{0,16},{16,0},{32,48},{48,32},{64,80},{80,64},{96,112},{112,96},{1... | collective-permute-start | bytes 4718600 | tf_op jit(solution)/shard_map/ppermute | solution.py:141
  6.0 1.5 %dynamic-slice_bitcast_fusion = bf16[4,12,32,512]{3,2,1,0:T(8,128)(2,1)S(1)} fusion(bf16[4,2,2,12,32,512]{5,4,3,2,1,0:T(8,128)(2,1)} %bitcast.61, s32[]{:T(128)S(6)} %select_n.90, s32[]{:T(128)S(6)} %select_n.94), kind=kLoop, calls=%fused_computation | loop fusion | bytes 3145736 | tf_op jit(solution)/shard_map/reshape | solution.py:167
  7.7 1.7 %collective-permute-done.1 = bf16[4,12,32,512]{3,2,1,0:T(8,128)(2,1)} collective-permute-done((bf16[4,12,32,512]{3,2,1,0:T(8,128)(2,1)}, bf16[4,12,32,512]{3,2,1,0:T(8,128)(2,1)}, u32[]{:S(2)}, u32[]{:S(2)}) %collective-permute-start.1) | collective-permute-done | bytes 1572896 | tf_op jit(solution)/shard_map/ppermute | solution.py:141
  9.4 2.4 %fusion.3 = (f16[12,32,512]{2,1,0:T(8,128)(2,1)}, f16[12,32,512]{2,1,0:T(8,128)(2,1)S(1)}) fusion(bf16[4,12,32,512]{3,2,1,0:T(8,128)(2,1)} %collective-permute-done.1, s32[]{:T(128)S(6)} %select_n.99, bf16[4,2,2,12,32,512]{5,4,3,2,1,0:T(8,128)(2,1)} %bitcast.62, s32[]{:T(128)S(6)} %select_n.93, s32[]{:T(128)S(6)} %select_n.92, s32[]{:T(128)S(6)} %select_n.97), kind=kLoop, calls=%fused_computation.7 | loop fusion | flops 1966080 | bytes 2359312 | tf_op jit(solution)/shard_map/convert_element_type | solution.py:149
  11.8 1.0 collective-permute-start.2
  12.8 1.7 %collective-permute-start.3 = (f16[12,32,512]{2,1,0:T(8,128)(2,1)}, f16[12,32,512]{2,1,0:T(8,128)(2,1)}, u32[]{:S(2)}, u32[]{:S(2)}) collective-permute-start(f16[12,32,512]{2,1,0:T(8,128)(2,1)} %get-tuple-element.13), channel_id=1, source_target_pairs={{0,64},{16,208},{32,96},{48,240},{64,0},{80,144},{96,32},{112,176}... | collective-permute-start | bytes 1179656 | tf_op jit(solution)/shard_map/ppermute | solution.py:141
  14.4 5.3 %collective-permute-done.2 = f16[12,32,512]{2,1,0:T(8,128)(2,1)} collective-permute-done((f16[12,32,512]{2,1,0:T(8,128)(2,1)S(1)}, f16[12,32,512]{2,1,0:T(8,128)(2,1)}, u32[]{:S(2)}, u32[]{:S(2)}) %collective-permute-start.2) | collective-permute-done | bytes 393248 | tf_op jit(solution)/shard_map/ppermute | solution.py:141
  19.7 1.4 %fusion.17 = f16[12,32,512]{2,1,0:T(8,128)(2,1)S(1)} fusion(f16[12,32,512]{2,1,0:T(8,128)(2,1)} %collective-permute-done.2, bf16[4,12,32,512]{3,2,1,0:T(8,128)(2,1)} %collective-permute-done.1, s32[]{:T(128)S(6)} %select_n.96, bf16[4,2,2,12,32,512]{5,4,3,2,1,0:T(8,128)(2,1)} %bitcast.63, s32[]{:T(128)S(6)} %select_n.93, s32[]{:T(128)S(6)} %select_n.92), kind=kLoop, calls=%fused_computation.27 | loop fusion | flops 1376256 | bytes 1572876 | tf_op jit(solution)/shard_map/convert_element_type | solution.py:149
  21.4 1.7 %fusion.12 = (f16[12,32,512]{2,1,0:T(8,128)(2,1)S(1)}, f16[12,32,512]{2,1,0:T(8,128)(2,1)S(1)}, f16[12,32,512]{2,1,0:T(8,128)(2,1)S(1)}) fusion(bf16[4,12,32,512]{3,2,1,0:T(8,128)(2,1)S(1)} %collective-permute-done, s32[]{:T(128)S(6)} %select_n.97, bf16[4,2,2,12,32,512]{5,4,3,2,1,0:T(8,128)(2,1)} %bitcast.64, s32[]{:T(128)S(6)} %select_n.90, ...), kind=kLoop, calls=%fused_computation.20 | loop fusion | flops 2949120 | bytes 3538964 | tf_op jit(solution)/shard_map/convert_element_type | solution.py:149
  23.2 2.2 %collective-permute-start.5 = (f16[12,32,512]{2,1,0:T(8,128)(2,1)S(1)}, f16[12,32,512]{2,1,0:T(8,128)(2,1)S(1)}, u32[]{:S(2)}, u32[]{:S(2)}) collective-permute-start(f16[12,32,512]{2,1,0:T(8,128)(2,1)S(1)} %get-tuple-element.15), channel_id=1, source_target_pairs={{0,128},{16,144},{32,160},{48,176},{64,192},{80,208},{96,224},{112... | collective-permute-start | bytes 1179656 | tf_op jit(solution)/shard_map/ppermute | solution.py:141
  25.4 1.7 %collective-permute-start.6 = (f16[12,32,512]{2,1,0:T(8,128)(2,1)S(1)}, f16[12,32,512]{2,1,0:T(8,128)(2,1)S(1)}, u32[]{:S(2)}, u32[]{:S(2)}) collective-permute-start(f16[12,32,512]{2,1,0:T(8,128)(2,1)S(1)} %get-tuple-element.17), channel_id=1, source_target_pairs={{0,64},{16,208},{32,96},{48,240},{64,0},{80,144},{96,32},{112,176}... | collective-permute-start | bytes 1179656 | tf_op jit(solution)/shard_map/ppermute | solution.py:141
  27.1 1.2 collective-permute-done.4
  28.3 1.6 %fusion.6 = f16[12,32,512]{2,1,0:T(8,128)(2,1)S(1)} fusion(f16[12,32,512]{2,1,0:T(8,128)(2,1)} %collective-permute-done.4, f16[12,32,512]{2,1,0:T(8,128)(2,1)} %collective-permute-done.3, bf16[4,12,32,512]{3,2,1,0:T(8,128)(2,1)} %collective-permute-done.1, s32[]{:T(128)S(6)} %select_n.87, bf16[4,2,2,12,32,512]{5,4,3,2,1,0:T(8,128)(2,1)} %bitcast.65, ...), kind=kLoop, calls=%fused_computation.11 | loop fusion | flops 1769472 | bytes 1966092 | tf_op jit(solution)/shard_map/convert_element_type | solution.py:149
  29.9 5.3 %collective-permute-start.8 = (f16[12,32,512]{2,1,0:T(8,128)(2,1)S(1)}, f16[12,32,512]{2,1,0:T(8,128)(2,1)S(1)}, u32[]{:S(2)}, u32[]{:S(2)}) collective-permute-start(f16[12,32,512]{2,1,0:T(8,128)(2,1)S(1)} %fusion.6), channel_id=1, source_target_pairs={{0,32},{16,48},{32,0},{48,16},{64,96},{80,112},{96,64},{112,80},{1... | collective-permute-start | bytes 1179656 | tf_op jit(solution)/shard_map/ppermute | solution.py:141
  35.3 1.3 %collective-permute-done.5 = f16[12,32,512]{2,1,0:T(8,128)(2,1)S(1)} collective-permute-done((f16[12,32,512]{2,1,0:T(8,128)(2,1)S(1)}, f16[12,32,512]{2,1,0:T(8,128)(2,1)S(1)}, u32[]{:S(2)}, u32[]{:S(2)}) %collective-permute-start.5) | collective-permute-done | bytes 393248 | tf_op jit(solution)/shard_map/ppermute | solution.py:141
  36.7 7.7 %collective-permute-done.7 = f16[12,32,512]{2,1,0:T(8,128)(2,1)S(1)} collective-permute-done((f16[12,32,512]{2,1,0:T(8,128)(2,1)S(1)}, f16[12,32,512]{2,1,0:T(8,128)(2,1)S(1)}, u32[]{:S(2)}, u32[]{:S(2)}) %collective-permute-start.7) | collective-permute-done | bytes 393248 | tf_op jit(solution)/shard_map/ppermute | solution.py:141
  44.4 1.5 %collective-permute-done.6 = f16[12,32,512]{2,1,0:T(8,128)(2,1)S(1)} collective-permute-done((f16[12,32,512]{2,1,0:T(8,128)(2,1)S(1)}, f16[12,32,512]{2,1,0:T(8,128)(2,1)S(1)}, u32[]{:S(2)}, u32[]{:S(2)}) %collective-permute-start.6) | collective-permute-done | bytes 393248 | tf_op jit(solution)/shard_map/ppermute | solution.py:141
  45.9 1.3 %fusion.1 = f32[12,32,512]{2,1,0:T(8,128)S(1)} fusion(f16[12,32,512]{2,1,0:T(8,128)(2,1)S(1)} %collective-permute-done.7, f16[12,32,512]{2,1,0:T(8,128)(2,1)S(1)} %collective-permute-done.6, f16[12,32,512]{2,1,0:T(8,128)(2,1)S(1)} %collective-permute-done.5, bf16[4,12,32,512]{3,2,1,0:T(8,128)(2,1)S(1)} %collective-permute-done, s32[]{:T(128)S(6)} %select_n.87, ...), kind=kLoop, calls=%fused_computation.4 | loop fusion | flops 1966080 | bytes 2752524 | tf_op jit(solution)/shard_map/add | solution.py:188
  47.4 0.6 shard_map.37
  48.0 32.2 %all_to_all.10.pieces_ref = bf16[16,2,32,512]{3,2,1,0:T(8,128)(2,1)S(1)} all-to-all(bf16[16,2,32,512]{3,2,1,0:T(8,128)(2,1)S(1)} %bitcast.58), channel_id=1, replica_groups=mesh['dp'=16,'grp'=16] {'grp'}, dimensions={0} | all-to-all | bytes 2097152 | tf_op jit(solution)/shard_map/all_to_all | solution.py:209
  80.2 10.1 %shard_map.38 = bf16[16,2,32,512]{3,2,1,0:T(8,128)(2,1)S(1)} custom-call(bf16[16,2,32,512]{3,2,1,0:T(8,128)(2,1)S(1)} %all_to_all.10.pieces_ref, f32[2,2,512,512]{3,2,1,0:T(8,128)} %bitcast.67), custom_call_target="tpu_custom_call" | custom-call | tf_op jit(solution)/shard_map/pallas_call | solution.py:106
  90.2 29.4 %all_to_all.11 = bf16[16,2,32,512]{3,2,1,0:T(8,128)(2,1)S(1)} all-to-all(bf16[16,2,32,512]{3,2,1,0:T(8,128)(2,1)S(1)} %shard_map.38), channel_id=1, replica_groups=mesh['dp'=16,'grp'=16] {'grp'}, dimensions={0} | all-to-all | bytes 2097152 | tf_op jit(solution)/shard_map/all_to_all | solution.py:211
  119.6 1.5 %shard_map.39 = f32[12,32,512]{2,1,0:T(8,128)} custom-call(s32[12]{0:T(128)S(1)} %multiply_add_fusion.index_ref, bf16[32,32,512]{2,1,0:T(8,128)(2,1)S(1)} %bitcast.59), custom_call_target="tpu_custom_call" | custom-call | tf_op jit(solution)/shard_map/pallas_call | solution.py:128
  (12 shorter events, 0.6 us)
Async XLA Ops:
  2.7 6.6 %collective-permute-start.1 = (bf16[4,12,32,512]{3,2,1,0:T(8,128)(2,1)}, bf16[4,12,32,512]{3,2,1,0:T(8,128)(2,1)}, u32[]{:S(2)}, u32[]{:S(2)}) collective-permute-start(bf16[4,12,32,512]{3,2,1,0:T(8,128)(2,1)} %dynamic-slice_bitcast_fusion.1), channel_id=1, source_target_pairs={{0,16},{16,0},{32,48},{48,32},{64,80},{80,64},{96,112},{112,96},{1... | collective-permute-start | bytes 4718600 | tf_op jit(solution)/shard_map/ppermute | solution.py:141
  7.5 13.9 %collective-permute-start = (bf16[4,12,32,512]{3,2,1,0:T(8,128)(2,1)S(1)}, bf16[4,12,32,512]{3,2,1,0:T(8,128)(2,1)S(1)}, u32[]{:S(2)}, u32[]{:S(2)}) collective-permute-start(bf16[4,12,32,512]{3,2,1,0:T(8,128)(2,1)S(1)} %dynamic-slice_bitcast_fusion), channel_id=1, source_target_pairs={{0,16},{16,0},{32,48},{48,32},{64,80},{80,64},{96,112},{112,96},{1... | collective-permute-start | bytes 4718600 | tf_op jit(solution)/shard_map/ppermute | solution.py:141
  7.6 13.6 %copy-start = (s32[1,12,1]{1,2,0:T(1,128)S(1)}, s32[1,12,1]{1,2,0:T(1,128)}, u32[]{:S(2)}) copy-start(s32[1,12,1]{1,2,0:T(1,128)} %param.4) | copy-start | bytes 148
  11.8 7.9 %collective-permute-start.2 = (f16[12,32,512]{2,1,0:T(8,128)(2,1)S(1)}, f16[12,32,512]{2,1,0:T(8,128)(2,1)}, u32[]{:S(2)}, u32[]{:S(2)}) collective-permute-start(f16[12,32,512]{2,1,0:T(8,128)(2,1)S(1)} %get-tuple-element.14), channel_id=1, source_target_pairs={{0,64},{16,208},{32,96},{48,240},{64,0},{80,144},{96,32},{112,176}... | collective-permute-start | bytes 1179656 | tf_op jit(solution)/shard_map/ppermute | solution.py:141
  12.8 14.3 %collective-permute-start.3 = (f16[12,32,512]{2,1,0:T(8,128)(2,1)}, f16[12,32,512]{2,1,0:T(8,128)(2,1)}, u32[]{:S(2)}, u32[]{:S(2)}) collective-permute-start(f16[12,32,512]{2,1,0:T(8,128)(2,1)} %get-tuple-element.13), channel_id=1, source_target_pairs={{0,64},{16,208},{32,96},{48,240},{64,0},{80,144},{96,32},{112,176}... | collective-permute-start | bytes 1179656 | tf_op jit(solution)/shard_map/ppermute | solution.py:141
  21.1 7.1 %collective-permute-start.4 = (f16[12,32,512]{2,1,0:T(8,128)(2,1)S(1)}, f16[12,32,512]{2,1,0:T(8,128)(2,1)}, u32[]{:S(2)}, u32[]{:S(2)}) collective-permute-start(f16[12,32,512]{2,1,0:T(8,128)(2,1)S(1)} %fusion.17), channel_id=1, source_target_pairs={{0,192},{16,80},{32,224},{48,112},{64,128},{80,16},{96,160},{112,4... | collective-permute-start | bytes 1179656 | tf_op jit(solution)/shard_map/ppermute | solution.py:141
  23.2 13.5 %collective-permute-start.5 = (f16[12,32,512]{2,1,0:T(8,128)(2,1)S(1)}, f16[12,32,512]{2,1,0:T(8,128)(2,1)S(1)}, u32[]{:S(2)}, u32[]{:S(2)}) collective-permute-start(f16[12,32,512]{2,1,0:T(8,128)(2,1)S(1)} %get-tuple-element.15), channel_id=1, source_target_pairs={{0,128},{16,144},{32,160},{48,176},{64,192},{80,208},{96,224},{112... | collective-permute-start | bytes 1179656 | tf_op jit(solution)/shard_map/ppermute | solution.py:141
  25.4 19.0 %collective-permute-start.7 = (f16[12,32,512]{2,1,0:T(8,128)(2,1)S(1)}, f16[12,32,512]{2,1,0:T(8,128)(2,1)S(1)}, u32[]{:S(2)}, u32[]{:S(2)}) collective-permute-start(f16[12,32,512]{2,1,0:T(8,128)(2,1)S(1)} %get-tuple-element.16), channel_id=1, source_target_pairs={{0,192},{16,80},{32,224},{48,112},{64,128},{80,16},{96,160},{112,4... | collective-permute-start | bytes 1179656 | tf_op jit(solution)/shard_map/ppermute | solution.py:141
  25.4 20.5 %collective-permute-start.6 = (f16[12,32,512]{2,1,0:T(8,128)(2,1)S(1)}, f16[12,32,512]{2,1,0:T(8,128)(2,1)S(1)}, u32[]{:S(2)}, u32[]{:S(2)}) collective-permute-start(f16[12,32,512]{2,1,0:T(8,128)(2,1)S(1)} %get-tuple-element.17), channel_id=1, source_target_pairs={{0,64},{16,208},{32,96},{48,240},{64,0},{80,144},{96,32},{112,176}... | collective-permute-start | bytes 1179656 | tf_op jit(solution)/shard_map/ppermute | solution.py:141
  29.9 17.3 %collective-permute-start.8 = (f16[12,32,512]{2,1,0:T(8,128)(2,1)S(1)}, f16[12,32,512]{2,1,0:T(8,128)(2,1)S(1)}, u32[]{:S(2)}, u32[]{:S(2)}) collective-permute-start(f16[12,32,512]{2,1,0:T(8,128)(2,1)S(1)} %fusion.6), channel_id=1, source_target_pairs={{0,32},{16,48},{32,0},{48,16},{64,96},{80,112},{96,64},{112,80},{1... | collective-permute-start | bytes 1179656 | tf_op jit(solution)/shard_map/ppermute | solution.py:141

commit v3 on v2

--- a/solution.py
+++ b/solution.py
@@ -27,23 +27,6 @@
 LAST = dp_perm(lambda y, z, c: (3 - y if c == 0 else y ^ 1, z, c))
 OTHER_Z = dp_perm(lambda y, z, c: (y, 1 - z, c))
 OPPOSITE = dp_perm(lambda y, z, c: (y ^ 2, z, c))
-NX, NLO = 4, 4
-
-
-def ring_perm():
-    pairs = []
-    for dp in range(NY * NZ * NC):
-        for grp in range(NX * NLO):
-            y, hi, c = dp // (NZ * NC), (dp // NC) % NZ, dp % NC
-            x, lo = grp // NLO, grp % NLO
-            ring = (hi * NLO + lo + (2 if c == 0 else -2)) % (NZ * NLO)
-            target = (y * NZ + ring // NLO) * NC + c
-            pairs.append((dp * NX * NLO + grp, target * NX * NLO + x * NLO + ring % NLO))
-    return pairs
-
-
-ALONG_Z = ring_perm()
-
 
 def root_coefficients():
     f0, f1 = 27.0 / 22.0, -5.0 / 22.0
@@ -172,16 +155,30 @@
         theirs = lax.dynamic_slice(other, (at_y, 0, 0, 0), (1, count, rows, width)).reshape(count, rows, width)
         return (wide(mine) + wide(theirs)) * SCALE
 
-    to_core1 = held(parts, 1, 1)
-    other1 = send(to_core1, CORE)
-    other0 = send(held(after(parts, to_core1), 0, 1), CORE)
-    first1 = coded(part(opposite, 1, other1)), coded(part(following, 1, other1))
+    def wanted(source, at_y):
+        at = (at_y, z ^ 1, c ^ 1, 0, 0, 0)
+        return lax.dynamic_slice(source, at, (1, 1, 1, count, rows, width)).reshape(1, count, rows, width)
+
+    def joined(at_y, other):
+        at = (at_y, z ^ 1, c, 0, 0, 0)
+        mine = lax.dynamic_slice(parts, at, (1, 1, 1, count, rows, width)).reshape(count, rows, width)
+        return (wide(mine) + wide(other[0])) * SCALE
+
+    early = wanted(parts, opposite), wanted(parts, preceding)
+    early1 = [send(value, CORE) for value in early]
+    source = after(parts, *early)
+    late = wanted(source, following), wanted(source, y)
+    late1 = [send(value, CORE) for value in late]
+    first1 = coded(joined(opposite, early1[0])), coded(joined(following, early1[1]))
     far1, near1 = (send(value, NEXT) for value in first1)
-    second1 = coded(part(preceding, 1, other1) + wide(far1))
+    to_core0 = held(after(parts, *late, *first1), 0, 1)
+    other0 = send(to_core0, CORE)
+    direct = [coded(part(opposite, 0, other0))]
+    second1 = coded(joined(preceding, after(late1[0], *direct)) + wide(far1))
     last1 = send(second1, LAST)
     other0 = after(other0, second1)
-    direct = [coded(part(at, 0, other0)) for at in (opposite, following, preceding)]
-    crossing = coded(part(y, 1, after(other1, *direct)) + (wide(near1) + wide(last1)))
+    direct += [coded(part(at, 0, other0)) for at in (following, preceding)]
+    crossing = coded(joined(y, after(late1[1], *direct)) + (wide(near1) + wide(last1)))
     crossed = send(crossing, OTHER_Z)
     along0 = [send(value, pairs) for value, pairs in zip(direct, (OPPOSITE, NEXT, LAST))]
     other0 = after(other0, crossing, *direct)

time: 121 us -> 118 us (0.975)
  waiting for transfers between devices: 18.7 us -> 16.5 us
    reshape x2 -> x1, local copies, waits for them, and re-layouts: 4.26 us -> 1.52 us  [held(): lax.dynamic_slice(source, at, (NY, 1, 1, count, rows, width))]
    reshape x0 -> x2, local copies, waits for them, and re-layouts: none -> 2.35 us  [wanted(): lax.dynamic_slice(source, at, (1, 1, 1, count, rows, width))]
    ppermute x9 -> x12, waiting for transfers between devices: 18.7 us -> 16.5 us  [send(): return lax.ppermute(array, 'dp', perm)]
    ppermute x9 -> x12, starting transfers between devices: 15.3 us -> 16.2 us  [send(): return lax.ppermute(array, 'dp', perm)]
    convert_element_type x4 -> x5, other arithmetic: 7.16 us -> 6.43 us  [coded(): return array.astype(jnp.float16)]
  transfers between devices with their start and end apart: 9 -> 12, of which waited for: 6 -> 7; matrix products, arithmetic and copies ran while one was open for 8% -> 7% of each run, Pallas kernels for 0% -> 0%
where the time goes in v3:
time: 118 us
  blocking collectives  60.6 us (51%)
  waiting for transfers between devices  16.5 us (14%)
  starting transfers between devices  16.2 us (14%)
  Pallas kernels  12.1 us (10%)
  other arithmetic  8.2 us (7%)
  local copies, waits for them, and re-layouts  3.87 us (3%)
    all_to_all x1, blocking collectives, body(): lax.all_to_all(outgoing, 'grp', split_axis=0, concat_axis=0, tiled=True)  31.9 us
    all_to_all x1, blocking collectives, body(): lax.all_to_all(result, 'grp', split_axis=0, concat_axis=0, tiled=True)  28.7 us
    ppermute x12, waiting for transfers between devices, send(): return lax.ppermute(array, 'dp', perm)  16.5 us
    ppermute x12, starting transfers between devices, send(): return lax.ppermute(array, 'dp', perm)  16.2 us
    pallas_call x1, Pallas kernels, directions(): pl.pallas_call(gram_kernel, in_specs=[pl.BlockSpec(memory_space=pltpu.VME...  10.1 us
    convert_element_type x5, other arithmetic, coded(): return array.astype(jnp.float16)  6.43 us
  transfers between devices with their start and end apart: 12, of which 7 were waited for; matrix products, arithmetic and copies ran while one was open for 7% of the time, Pallas kernels for 0%

profile of v3, /device:TPU:1, one launch (start us, length us, event | category | flops | bytes accessed | tf_op | source)
XLA Modules:
  0.0 117.6 jit_solution(6537107595581090979)
XLA Ops:
  0.0 1.2 %dynamic-slice_bitcast_fusion.3 = (bf16[1,12,32,512]{3,2,1,0:T(8,128)(2,1)S(1)}, bf16[1,12,32,512]{3,2,1,0:T(8,128)(2,1)S(1)}) fusion(bf16[4,2,2,12,32,512]{5,4,3,2,1,0:T(8,128)(2,1)} %bitcast.66, s32[]{:T(128)S(6)} %select_n.103, s32[]{:T(128)S(6)} %select_n.100, s32[]{:T(128)S(6)} %select_n.101, s32[]{:T(128)S(6)} %select_n.99), kind=kLoop, calls=%fused_computation.30 | loop fusion | bytes 1572880 | tf_op jit(solution)/shard_map/reshape | solution.py:160
  1.2 3.3 %collective-permute-start = (bf16[1,12,32,512]{3,2,1,0:T(8,128)(2,1)S(1)}, bf16[1,12,32,512]{3,2,1,0:T(8,128)(2,1)S(1)}, u32[]{:S(2)}, u32[]{:S(2)}) collective-permute-start(bf16[1,12,32,512]{3,2,1,0:T(8,128)(2,1)S(1)} %get-tuple-element.24), channel_id=1, source_target_pairs={{0,16},{16,0},{32,48},{48,32},{64,80},{80,64},{96,112},{112,96},{1... | collective-permute-start | bytes 1179656 | tf_op jit(solution)/shard_map/ppermute | solution.py:124
  4.6 1.2 dynamic-slice_bitcast_fusion.1
  5.9 0.6 collective-permute-done.1
  6.4 1.4 %fusion.15 = (f16[12,32,512]{2,1,0:T(8,128)(2,1)S(1)}, f16[12,32,512]{2,1,0:T(8,128)(2,1)S(1)}) fusion(bf16[1,12,32,512]{3,2,1,0:T(8,128)(2,1)S(1)} %collective-permute-done.1, bf16[4,2,2,12,32,512]{5,4,3,2,1,0:T(8,128)(2,1)} %bitcast.68, s32[]{:T(128)S(6)} %select_n.105, s32[]{:T(128)S(6)} %select_n.100, s32[]{:T(128)S(6)} %select_n.98, ...), kind=kLoop, calls=%fused_computation.23 | loop fusion | flops 1966080 | bytes 2359312 | tf_op jit(solution)/shard_map/convert_element_type | solution.py:132
  7.8 1.5 %dynamic-slice_bitcast_fusion = bf16[4,12,32,512]{3,2,1,0:T(8,128)(2,1)S(1)} fusion(bf16[4,2,2,12,32,512]{5,4,3,2,1,0:T(8,128)(2,1)} %bitcast.69, s32[]{:T(128)S(6)} %select_n.96, s32[]{:T(128)S(6)} %select_n.101), kind=kLoop, calls=%fused_computation | loop fusion | bytes 3145736 | tf_op jit(solution)/shard_map/reshape | solution.py:150
  10.0 1.0 collective-permute-start.4
  11.0 1.7 %collective-permute-start.6 = (f16[12,32,512]{2,1,0:T(8,128)(2,1)S(1)}, f16[12,32,512]{2,1,0:T(8,128)(2,1)S(1)}, u32[]{:S(2)}, u32[]{:S(2)}) collective-permute-start(f16[12,32,512]{2,1,0:T(8,128)(2,1)S(1)} %get-tuple-element.19), channel_id=1, source_target_pairs={{0,64},{16,208},{32,96},{48,240},{64,0},{80,144},{96,32},{112,176}... | collective-permute-start | bytes 1179656 | tf_op jit(solution)/shard_map/ppermute | solution.py:124
  12.9 1.1 fusion.13
  14.0 3.8 %collective-permute-done.4 = f16[12,32,512]{2,1,0:T(8,128)(2,1)S(1)} collective-permute-done((f16[12,32,512]{2,1,0:T(8,128)(2,1)S(1)}, f16[12,32,512]{2,1,0:T(8,128)(2,1)S(1)}, u32[]{:S(2)}, u32[]{:S(2)}) %collective-permute-start.4) | collective-permute-done | bytes 393248 | tf_op jit(solution)/shard_map/ppermute | solution.py:124
  17.8 1.2 %fusion.11 = f16[12,32,512]{2,1,0:T(8,128)(2,1)S(1)} fusion(f16[12,32,512]{2,1,0:T(8,128)(2,1)S(1)} %collective-permute-done.4, bf16[1,12,32,512]{3,2,1,0:T(8,128)(2,1)S(1)} %collective-permute-done.3, bf16[4,2,2,12,32,512]{5,4,3,2,1,0:T(8,128)(2,1)} %bitcast.71, s32[]{:T(128)S(6)} %select_n.103, s32[]{:T(128)S(6)} %select_n.100, s32[]{:T(128)S(6)} %select_n.98), kind=kLoop, calls=%fused_computation.17 | loop fusion | flops 1376256 | bytes 1572876 | tf_op jit(solution)/shard_map/convert_element_type | solution.py:132
  19.3 2.2 %collective-permute-start.8 = (f16[12,32,512]{2,1,0:T(8,128)(2,1)S(1)}, f16[12,32,512]{2,1,0:T(8,128)(2,1)S(1)}, u32[]{:S(2)}, u32[]{:S(2)}) collective-permute-start(f16[12,32,512]{2,1,0:T(8,128)(2,1)S(1)} %fusion.13), channel_id=1, source_target_pairs={{0,128},{16,144},{32,160},{48,176},{64,192},{80,208},{96,224},{112... | collective-permute-start | bytes 1179656 | tf_op jit(solution)/shard_map/ppermute | solution.py:124
  21.5 1.4 %fusion.8 = (f16[12,32,512]{2,1,0:T(8,128)(2,1)S(1)}, f16[12,32,512]{2,1,0:T(8,128)(2,1)S(1)}) fusion(bf16[4,12,32,512]{3,2,1,0:T(8,128)(2,1)S(1)} %collective-permute-done.2, s32[]{:T(128)S(6)} %select_n.105, bf16[4,2,2,12,32,512]{5,4,3,2,1,0:T(8,128)(2,1)} %bitcast.72, s32[]{:T(128)S(6)} %select_n.96, s32[]{:T(128)S(6)} %select_n.98, s32[]{:T(128)S(6)} %select_n.103), kind=kLoop, calls=%fused_computation.13 | loop fusion | flops 1966080 | bytes 2359312 | tf_op jit(solution)/shard_map/convert_element_type | solution.py:132
  23.1 1.8 %collective-permute-start.9 = (f16[12,32,512]{2,1,0:T(8,128)(2,1)S(1)}, f16[12,32,512]{2,1,0:T(8,128)(2,1)S(1)}, u32[]{:S(2)}, u32[]{:S(2)}) collective-permute-start(f16[12,32,512]{2,1,0:T(8,128)(2,1)S(1)} %get-tuple-element.17), channel_id=1, source_target_pairs={{0,64},{16,208},{32,96},{48,240},{64,0},{80,144},{96,32},{112,176}... | collective-permute-start | bytes 1179656 | tf_op jit(solution)/shard_map/ppermute | solution.py:124
  24.8 2.5 %collective-permute-done.7 = f16[12,32,512]{2,1,0:T(8,128)(2,1)S(1)} collective-permute-done((f16[12,32,512]{2,1,0:T(8,128)(2,1)S(1)}, f16[12,32,512]{2,1,0:T(8,128)(2,1)S(1)}, u32[]{:S(2)}, u32[]{:S(2)}) %collective-permute-start.7) | collective-permute-done | bytes 393248 | tf_op jit(solution)/shard_map/ppermute | solution.py:124
  27.3 1.3 %fusion.4 = f16[12,32,512]{2,1,0:T(8,128)(2,1)S(1)} fusion(f16[12,32,512]{2,1,0:T(8,128)(2,1)S(1)} %collective-permute-done.7, f16[12,32,512]{2,1,0:T(8,128)(2,1)S(1)} %collective-permute-done.6, bf16[1,12,32,512]{3,2,1,0:T(8,128)(2,1)S(1)} %collective-permute-done.5, bf16[4,2,2,12,32,512]{5,4,3,2,1,0:T(8,128)(2,1)} %bitcast.73, s32[]{:T(128)S(6)} %select_n.93, ...), kind=kLoop, calls=%fused_computation.7 | loop fusion | flops 1769472 | bytes 1966092 | tf_op jit(solution)/shard_map/convert_element_type | solution.py:132
  28.6 5.3 %collective-permute-start.11 = (f16[12,32,512]{2,1,0:T(8,128)(2,1)S(1)}, f16[12,32,512]{2,1,0:T(8,128)(2,1)S(1)}, u32[]{:S(2)}, u32[]{:S(2)}) collective-permute-start(f16[12,32,512]{2,1,0:T(8,128)(2,1)S(1)} %fusion.4), channel_id=1, source_target_pairs={{0,32},{16,48},{32,0},{48,16},{64,96},{80,112},{96,64},{112,80},{1... | collective-permute-start | bytes 1179656 | tf_op jit(solution)/shard_map/ppermute | solution.py:124
  34.0 9.1 %collective-permute-done.10 = f16[12,32,512]{2,1,0:T(8,128)(2,1)S(1)} collective-permute-done((f16[12,32,512]{2,1,0:T(8,128)(2,1)S(1)}, f16[12,32,512]{2,1,0:T(8,128)(2,1)S(1)}, u32[]{:S(2)}, u32[]{:S(2)}) %collective-permute-start.10) | collective-permute-done | bytes 393248 | tf_op jit(solution)/shard_map/ppermute | solution.py:124
  43.3 1.3 %fusion.1 = f32[12,32,512]{2,1,0:T(8,128)S(1)} fusion(f16[12,32,512]{2,1,0:T(8,128)(2,1)S(1)} %collective-permute-done.10, f16[12,32,512]{2,1,0:T(8,128)(2,1)S(1)} %collective-permute-done.9, f16[12,32,512]{2,1,0:T(8,128)(2,1)S(1)} %collective-permute-done.8, bf16[4,12,32,512]{3,2,1,0:T(8,128)(2,1)S(1)} %collective-permute-done.2, s32[]{:T(128)S(6)} %select_n.93, ...), kind=kLoop, calls=%fused_computation.3 | loop fusion | flops 1966080 | bytes 2752524 | tf_op jit(solution)/shard_map/add | solution.py:185
  44.8 0.6 shard_map.37
  45.4 31.9 %all_to_all.10.pieces_ref = bf16[16,2,32,512]{3,2,1,0:T(8,128)(2,1)S(1)} all-to-all(bf16[16,2,32,512]{3,2,1,0:T(8,128)(2,1)S(1)} %bitcast.64), channel_id=1, replica_groups=mesh['dp'=16,'grp'=16] {'grp'}, dimensions={0} | all-to-all | bytes 2097152 | tf_op jit(solution)/shard_map/all_to_all | solution.py:206
  77.3 10.1 %shard_map.38 = bf16[16,2,32,512]{3,2,1,0:T(8,128)(2,1)S(1)} custom-call(bf16[16,2,32,512]{3,2,1,0:T(8,128)(2,1)S(1)} %all_to_all.10.pieces_ref, f32[2,2,512,512]{3,2,1,0:T(8,128)} %bitcast.75), custom_call_target="tpu_custom_call" | custom-call | tf_op jit(solution)/shard_map/pallas_call | solution.py:89
  87.4 28.7 %all_to_all.11 = bf16[16,2,32,512]{3,2,1,0:T(8,128)(2,1)S(1)} all-to-all(bf16[16,2,32,512]{3,2,1,0:T(8,128)(2,1)S(1)} %shard_map.38), channel_id=1, replica_groups=mesh['dp'=16,'grp'=16] {'grp'}, dimensions={0} | all-to-all | bytes 2097152 | tf_op jit(solution)/shard_map/all_to_all | solution.py:208
  116.1 1.5 %shard_map.39 = f32[12,32,512]{2,1,0:T(8,128)} custom-call(s32[12]{0:T(128)S(1)} %multiply_add_fusion.index_ref, bf16[32,32,512]{2,1,0:T(8,128)(2,1)S(1)} %bitcast.65), custom_call_target="tpu_custom_call" | custom-call | tf_op jit(solution)/shard_map/pallas_call | solution.py:111
  (20 shorter events, 1.9 us)
Async XLA Ops:
  0.0 19.1 %copy-start = (s32[1,12,1]{1,2,0:T(1,128)S(1)}, s32[1,12,1]{1,2,0:T(1,128)}, u32[]{:S(2)}) copy-start(s32[1,12,1]{1,2,0:T(1,128)} %param.4) | copy-start | bytes 148
  1.2 4.7 %collective-permute-start = (bf16[1,12,32,512]{3,2,1,0:T(8,128)(2,1)S(1)}, bf16[1,12,32,512]{3,2,1,0:T(8,128)(2,1)S(1)}, u32[]{:S(2)}, u32[]{:S(2)}) collective-permute-start(bf16[1,12,32,512]{3,2,1,0:T(8,128)(2,1)S(1)} %get-tuple-element.24), channel_id=1, source_target_pairs={{0,16},{16,0},{32,48},{48,32},{64,80},{80,64},{96,112},{112,96},{1... | collective-permute-start | bytes 1179656 | tf_op jit(solution)/shard_map/ppermute | solution.py:124
  4.5 1.9 %collective-permute-start.1 = (bf16[1,12,32,512]{3,2,1,0:T(8,128)(2,1)S(1)}, bf16[1,12,32,512]{3,2,1,0:T(8,128)(2,1)S(1)}, u32[]{:S(2)}, u32[]{:S(2)}) collective-permute-start(bf16[1,12,32,512]{3,2,1,0:T(8,128)(2,1)S(1)} %get-tuple-element.23), channel_id=1, source_target_pairs={{0,16},{16,0},{32,48},{48,32},{64,80},{80,64},{96,112},{112,96},{1... | collective-permute-start | bytes 1179656 | tf_op jit(solution)/shard_map/ppermute | solution.py:124
  9.4 3.5 %collective-permute-start.2 = (bf16[4,12,32,512]{3,2,1,0:T(8,128)(2,1)S(1)}, bf16[4,12,32,512]{3,2,1,0:T(8,128)(2,1)S(1)}, u32[]{:S(2)}, u32[]{:S(2)}) collective-permute-start(bf16[4,12,32,512]{3,2,1,0:T(8,128)(2,1)S(1)} %dynamic-slice_bitcast_fusion), channel_id=1, source_target_pairs={{0,16},{16,0},{32,48},{48,32},{64,80},{80,64},{96,112},{112,96},{1... | collective-permute-start | bytes 4718600 | tf_op jit(solution)/shard_map/ppermute | solution.py:124
  9.8 4.2 %collective-permute-start.3 = (bf16[1,12,32,512]{3,2,1,0:T(8,128)(2,1)S(1)}, bf16[1,12,32,512]{3,2,1,0:T(8,128)(2,1)S(1)}, u32[]{:S(2)}, u32[]{:S(2)}) collective-permute-start(bf16[1,12,32,512]{3,2,1,0:T(8,128)(2,1)S(1)} %get-tuple-element.22), channel_id=1, source_target_pairs={{0,16},{16,0},{32,48},{48,32},{64,80},{80,64},{96,112},{112,96},{1... | collective-permute-start | bytes 1179656 | tf_op jit(solution)/shard_map/ppermute | solution.py:124
  10.0 7.8 %collective-permute-start.4 = (f16[12,32,512]{2,1,0:T(8,128)(2,1)S(1)}, f16[12,32,512]{2,1,0:T(8,128)(2,1)S(1)}, u32[]{:S(2)}, u32[]{:S(2)}) collective-permute-start(f16[12,32,512]{2,1,0:T(8,128)(2,1)S(1)} %get-tuple-element.20), channel_id=1, source_target_pairs={{0,64},{16,208},{32,96},{48,240},{64,0},{80,144},{96,32},{112,176}... | collective-permute-start | bytes 1179656 | tf_op jit(solution)/shard_map/ppermute | solution.py:124
  11.0 12.1 %collective-permute-start.5 = (bf16[1,12,32,512]{3,2,1,0:T(8,128)(2,1)S(1)}, bf16[1,12,32,512]{3,2,1,0:T(8,128)(2,1)S(1)}, u32[]{:S(2)}, u32[]{:S(2)}) collective-permute-start(bf16[1,12,32,512]{3,2,1,0:T(8,128)(2,1)S(1)} %get-tuple-element.21), channel_id=1, source_target_pairs={{0,16},{16,0},{32,48},{48,32},{64,80},{80,64},{96,112},{112,96},{1... | collective-permute-start | bytes 1179656 | tf_op jit(solution)/shard_map/ppermute | solution.py:124
  11.0 13.9 %collective-permute-start.6 = (f16[12,32,512]{2,1,0:T(8,128)(2,1)S(1)}, f16[12,32,512]{2,1,0:T(8,128)(2,1)S(1)}, u32[]{:S(2)}, u32[]{:S(2)}) collective-permute-start(f16[12,32,512]{2,1,0:T(8,128)(2,1)S(1)} %get-tuple-element.19), channel_id=1, source_target_pairs={{0,64},{16,208},{32,96},{48,240},{64,0},{80,144},{96,32},{112,176}... | collective-permute-start | bytes 1179656 | tf_op jit(solution)/shard_map/ppermute | solution.py:124
  19.0 8.3 %collective-permute-start.7 = (f16[12,32,512]{2,1,0:T(8,128)(2,1)S(1)}, f16[12,32,512]{2,1,0:T(8,128)(2,1)S(1)}, u32[]{:S(2)}, u32[]{:S(2)}) collective-permute-start(f16[12,32,512]{2,1,0:T(8,128)(2,1)S(1)} %fusion.11), channel_id=1, source_target_pairs={{0,192},{16,80},{32,224},{48,112},{64,128},{80,16},{96,160},{112,4... | collective-permute-start | bytes 1179656 | tf_op jit(solution)/shard_map/ppermute | solution.py:124
  19.3 24.0 %collective-permute-start.8 = (f16[12,32,512]{2,1,0:T(8,128)(2,1)S(1)}, f16[12,32,512]{2,1,0:T(8,128)(2,1)S(1)}, u32[]{:S(2)}, u32[]{:S(2)}) collective-permute-start(f16[12,32,512]{2,1,0:T(8,128)(2,1)S(1)} %fusion.13), channel_id=1, source_target_pairs={{0,128},{16,144},{32,160},{48,176},{64,192},{80,208},{96,224},{112... | collective-permute-start | bytes 1179656 | tf_op jit(solution)/shard_map/ppermute | solution.py:124
  22.9 20.1 %collective-permute-start.10 = (f16[12,32,512]{2,1,0:T(8,128)(2,1)S(1)}, f16[12,32,512]{2,1,0:T(8,128)(2,1)S(1)}, u32[]{:S(2)}, u32[]{:S(2)}) collective-permute-start(f16[12,32,512]{2,1,0:T(8,128)(2,1)S(1)} %get-tuple-element.18), channel_id=1, source_target_pairs={{0,192},{16,80},{32,224},{48,112},{64,128},{80,16},{96,160},{112,4... | collective-permute-start | bytes 1179656 | tf_op jit(solution)/shard_map/ppermute | solution.py:124
  23.1 20.2 %collective-permute-start.9 = (f16[12,32,512]{2,1,0:T(8,128)(2,1)S(1)}, f16[12,32,512]{2,1,0:T(8,128)(2,1)S(1)}, u32[]{:S(2)}, u32[]{:S(2)}) collective-permute-start(f16[12,32,512]{2,1,0:T(8,128)(2,1)S(1)} %get-tuple-element.17), channel_id=1, source_target_pairs={{0,64},{16,208},{32,96},{48,240},{64,0},{80,144},{96,32},{112,176}... | collective-permute-start | bytes 1179656 | tf_op jit(solution)/shard_map/ppermute | solution.py:124
  28.6 16.0 %collective-permute-start.11 = (f16[12,32,512]{2,1,0:T(8,128)(2,1)S(1)}, f16[12,32,512]{2,1,0:T(8,128)(2,1)S(1)}, u32[]{:S(2)}, u32[]{:S(2)}) collective-permute-start(f16[12,32,512]{2,1,0:T(8,128)(2,1)S(1)} %fusion.4), channel_id=1, source_target_pairs={{0,32},{16,48},{32,0},{48,16},{64,96},{80,112},{96,64},{112,80},{1... | collective-permute-start | bytes 1179656 | tf_op jit(solution)/shard_map/ppermute | solution.py:124

commit v4 on v3

--- a/solution.py
+++ b/solution.py
@@ -120,6 +120,40 @@
     )(index, array)
 
 
+def fetch_kernel(index_ref, in_ref, out_ref, taken, widened, arrived, written):
+    count = out_ref.shape[0]
+    loads = [pltpu.make_async_copy(in_ref.at[index_ref[k]], taken.at[k], arrived.at[k]) for k in range(count)]
+    stores = [pltpu.make_async_copy(widened.at[k], out_ref.at[k], written.at[k]) for k in range(count)]
+    for load in loads:
+        load.start()
+    for k in range(count):
+        loads[k].wait()
+        widened[k] = taken[k].astype(widened.dtype)
+        stores[k].start()
+    for store in stores:
+        store.wait()
+
+
+def fetch(index, array, dtype):
+    count, block = index.shape[0], array.shape[1:]
+    return pl.pallas_call(
+        fetch_kernel,
+        in_specs=[
+            pl.BlockSpec(memory_space=pltpu.SMEM),
+            pl.BlockSpec(memory_space=pl.ANY),
+        ],
+        out_specs=pl.BlockSpec(memory_space=pl.ANY),
+        out_shape=jax.ShapeDtypeStruct((count,) + block, dtype),
+        scratch_shapes=[
+            pltpu.VMEM((count,) + block, array.dtype),
+            pltpu.VMEM((count,) + block, dtype),
+            pltpu.SemaphoreType.DMA((count,)),
+            pltpu.SemaphoreType.DMA((count,)),
+        ],
+        compiler_params=pltpu.CompilerParams(vmem_limit_bytes=16 * MIB),
+    )(index, array)
+
+
 def send(array, perm):
     return lax.ppermute(array, "dp", perm)
 
@@ -206,7 +240,7 @@
     pieces = lax.all_to_all(outgoing, "grp", split_axis=0, concat_axis=0, tiled=True)
     result = directions(pieces, prev_stats[0, 0])
     back = lax.all_to_all(result, "grp", split_axis=0, concat_axis=0, tiled=True)
-    return pick(place, back.reshape(groups * places, rows, width), jnp.float32)
+    return fetch(place, back.reshape(groups * places, rows, width), jnp.float32)
 
 
 def solution(mesh):

time: 118 us -> 119 us (level)
    pallas_call x0 -> x1, Pallas kernels: none -> 2.14 us  [fetch(): pl.pallas_call(fetch_kernel, in_specs=[pl.BlockSpec(memory_space=pltpu.SM...]
    pallas_call x2 -> x1, Pallas kernels: 2.09 us -> 0.61 us  [pick(): pl.pallas_call(pick_kernel, in_specs=[pl.BlockSpec(memory_space=pltpu.SME...]
where the time goes in v4:
time: 119 us; the launch traced here: 118 us
  blocking collectives  60.6 us (51%)
  waiting for transfers between devices  16.5 us (14%)
  starting transfers between devices  16.2 us (14%)
  Pallas kernels  12.8 us (11%)
  other arithmetic  8.2 us (7%)
  local copies, waits for them, and re-layouts  3.87 us (3%)
    all_to_all x1, blocking collectives, body(): lax.all_to_all(outgoing, 'grp', split_axis=0, concat_axis=0, tiled=True)  31.9 us
    all_to_all x1, blocking collectives, body(): lax.all_to_all(result, 'grp', split_axis=0, concat_axis=0, tiled=True)  28.7 us
    ppermute x12, waiting for transfers between devices, send(): return lax.ppermute(array, 'dp', perm)  16.5 us
    ppermute x12, starting transfers between devices, send(): return lax.ppermute(array, 'dp', perm)  16.2 us
    pallas_call x1, Pallas kernels, directions(): pl.pallas_call(gram_kernel, in_specs=[pl.BlockSpec(memory_space=pltpu.VME...  10.1 us
    convert_element_type x5, other arithmetic, coded(): return array.astype(jnp.float16)  6.43 us
  transfers between devices with their start and end apart: 12, of which 7 were waited for; matrix products, arithmetic and copies ran while one was open for 7% of the time, Pallas kernels for 0%

profile of v4, /device:TPU:1, one launch (start us, length us, event | category | flops | bytes accessed | tf_op | source)
XLA Modules:
  0.0 118.4 jit_solution(10152019179825994325)
XLA Ops:
  0.0 1.2 dynamic-slice_bitcast_fusion.3
  1.2 3.3 %collective-permute-start = (bf16[1,12,32,512]{3,2,1,0:T(8,128)(2,1)S(1)}, bf16[1,12,32,512]{3,2,1,0:T(8,128)(2,1)S(1)}, u32[]{:S(2)}, u32[]{:S(2)}) collective-permute-start(bf16[1,12,32,512]{3,2,1,0:T(8,128)(2,1)S(1)} %get-tuple-element.24), channel_id=1, source_target_pairs={{0,16},{16,0},{32,48},{48,32},{64,80},{80,64},{96,112},{112,96},{1... | collective-permute-start | bytes 1179656 | tf_op jit(solution)/shard_map/ppermute | solution.py:158
  4.6 1.2 dynamic-slice_bitcast_fusion.1
  5.9 0.6 collective-permute-done.1
  6.4 1.4 %fusion.15 = (f16[12,32,512]{2,1,0:T(8,128)(2,1)S(1)}, f16[12,32,512]{2,1,0:T(8,128)(2,1)S(1)}) fusion(bf16[1,12,32,512]{3,2,1,0:T(8,128)(2,1)S(1)} %collective-permute-done.1, bf16[4,2,2,12,32,512]{5,4,3,2,1,0:T(8,128)(2,1)} %bitcast.68, s32[]{:T(128)S(6)} %select_n.105, s32[]{:T(128)S(6)} %select_n.100, s32[]{:T(128)S(6)} %select_n.98, ...), kind=kLoop, calls=%fused_computation.23 | loop fusion | flops 1966080 | bytes 2359312 | tf_op jit(solution)/shard_map/convert_element_type | solution.py:166
  7.8 1.5 %dynamic-slice_bitcast_fusion = bf16[4,12,32,512]{3,2,1,0:T(8,128)(2,1)S(1)} fusion(bf16[4,2,2,12,32,512]{5,4,3,2,1,0:T(8,128)(2,1)} %bitcast.69, s32[]{:T(128)S(6)} %select_n.96, s32[]{:T(128)S(6)} %select_n.101), kind=kLoop, calls=%fused_computation | loop fusion | bytes 3145736 | tf_op jit(solution)/shard_map/reshape | solution.py:184
  10.0 1.0 collective-permute-start.4
  11.0 1.7 %collective-permute-start.6 = (f16[12,32,512]{2,1,0:T(8,128)(2,1)S(1)}, f16[12,32,512]{2,1,0:T(8,128)(2,1)S(1)}, u32[]{:S(2)}, u32[]{:S(2)}) collective-permute-start(f16[12,32,512]{2,1,0:T(8,128)(2,1)S(1)} %get-tuple-element.19), channel_id=1, source_target_pairs={{0,64},{16,208},{32,96},{48,240},{64,0},{80,144},{96,32},{112,176}... | collective-permute-start | bytes 1179656 | tf_op jit(solution)/shard_map/ppermute | solution.py:158
  12.9 1.1 fusion.13
  14.0 3.8 %collective-permute-done.4 = f16[12,32,512]{2,1,0:T(8,128)(2,1)S(1)} collective-permute-done((f16[12,32,512]{2,1,0:T(8,128)(2,1)S(1)}, f16[12,32,512]{2,1,0:T(8,128)(2,1)S(1)}, u32[]{:S(2)}, u32[]{:S(2)}) %collective-permute-start.4) | collective-permute-done | bytes 393248 | tf_op jit(solution)/shard_map/ppermute | solution.py:158
  17.8 1.2 %fusion.11 = f16[12,32,512]{2,1,0:T(8,128)(2,1)S(1)} fusion(f16[12,32,512]{2,1,0:T(8,128)(2,1)S(1)} %collective-permute-done.4, bf16[1,12,32,512]{3,2,1,0:T(8,128)(2,1)S(1)} %collective-permute-done.3, bf16[4,2,2,12,32,512]{5,4,3,2,1,0:T(8,128)(2,1)} %bitcast.71, s32[]{:T(128)S(6)} %select_n.103, s32[]{:T(128)S(6)} %select_n.100, s32[]{:T(128)S(6)} %select_n.98), kind=kLoop, calls=%fused_computation.17 | loop fusion | flops 1376256 | bytes 1572876 | tf_op jit(solution)/shard_map/convert_element_type | solution.py:166
  19.3 2.2 %collective-permute-start.8 = (f16[12,32,512]{2,1,0:T(8,128)(2,1)S(1)}, f16[12,32,512]{2,1,0:T(8,128)(2,1)S(1)}, u32[]{:S(2)}, u32[]{:S(2)}) collective-permute-start(f16[12,32,512]{2,1,0:T(8,128)(2,1)S(1)} %fusion.13), channel_id=1, source_target_pairs={{0,128},{16,144},{32,160},{48,176},{64,192},{80,208},{96,224},{112... | collective-permute-start | bytes 1179656 | tf_op jit(solution)/shard_map/ppermute | solution.py:158
  21.5 1.4 %fusion.8 = (f16[12,32,512]{2,1,0:T(8,128)(2,1)S(1)}, f16[12,32,512]{2,1,0:T(8,128)(2,1)S(1)}) fusion(bf16[4,12,32,512]{3,2,1,0:T(8,128)(2,1)S(1)} %collective-permute-done.2, s32[]{:T(128)S(6)} %select_n.105, bf16[4,2,2,12,32,512]{5,4,3,2,1,0:T(8,128)(2,1)} %bitcast.72, s32[]{:T(128)S(6)} %select_n.96, s32[]{:T(128)S(6)} %select_n.98, s32[]{:T(128)S(6)} %select_n.103), kind=kLoop, calls=%fused_computation.13 | loop fusion | flops 1966080 | bytes 2359312 | tf_op jit(solution)/shard_map/convert_element_type | solution.py:166
  23.1 1.8 %collective-permute-start.9 = (f16[12,32,512]{2,1,0:T(8,128)(2,1)S(1)}, f16[12,32,512]{2,1,0:T(8,128)(2,1)S(1)}, u32[]{:S(2)}, u32[]{:S(2)}) collective-permute-start(f16[12,32,512]{2,1,0:T(8,128)(2,1)S(1)} %get-tuple-element.17), channel_id=1, source_target_pairs={{0,64},{16,208},{32,96},{48,240},{64,0},{80,144},{96,32},{112,176}... | collective-permute-start | bytes 1179656 | tf_op jit(solution)/shard_map/ppermute | solution.py:158
  24.8 2.5 %collective-permute-done.7 = f16[12,32,512]{2,1,0:T(8,128)(2,1)S(1)} collective-permute-done((f16[12,32,512]{2,1,0:T(8,128)(2,1)S(1)}, f16[12,32,512]{2,1,0:T(8,128)(2,1)S(1)}, u32[]{:S(2)}, u32[]{:S(2)}) %collective-permute-start.7) | collective-permute-done | bytes 393248 | tf_op jit(solution)/shard_map/ppermute | solution.py:158
  27.3 1.3 %fusion.4 = f16[12,32,512]{2,1,0:T(8,128)(2,1)S(1)} fusion(f16[12,32,512]{2,1,0:T(8,128)(2,1)S(1)} %collective-permute-done.7, f16[12,32,512]{2,1,0:T(8,128)(2,1)S(1)} %collective-permute-done.6, bf16[1,12,32,512]{3,2,1,0:T(8,128)(2,1)S(1)} %collective-permute-done.5, bf16[4,2,2,12,32,512]{5,4,3,2,1,0:T(8,128)(2,1)} %bitcast.73, s32[]{:T(128)S(6)} %select_n.93, ...), kind=kLoop, calls=%fused_computation.7 | loop fusion | flops 1769472 | bytes 1966092 | tf_op jit(solution)/shard_map/convert_element_type | solution.py:166
  28.6 5.3 %collective-permute-start.11 = (f16[12,32,512]{2,1,0:T(8,128)(2,1)S(1)}, f16[12,32,512]{2,1,0:T(8,128)(2,1)S(1)}, u32[]{:S(2)}, u32[]{:S(2)}) collective-permute-start(f16[12,32,512]{2,1,0:T(8,128)(2,1)S(1)} %fusion.4), channel_id=1, source_target_pairs={{0,32},{16,48},{32,0},{48,16},{64,96},{80,112},{96,64},{112,80},{1... | collective-permute-start | bytes 1179656 | tf_op jit(solution)/shard_map/ppermute | solution.py:158
  34.0 9.1 %collective-permute-done.10 = f16[12,32,512]{2,1,0:T(8,128)(2,1)S(1)} collective-permute-done((f16[12,32,512]{2,1,0:T(8,128)(2,1)S(1)}, f16[12,32,512]{2,1,0:T(8,128)(2,1)S(1)}, u32[]{:S(2)}, u32[]{:S(2)}) %collective-permute-start.10) | collective-permute-done | bytes 393248 | tf_op jit(solution)/shard_map/ppermute | solution.py:158
  43.3 1.3 %fusion.1 = f32[12,32,512]{2,1,0:T(8,128)S(1)} fusion(f16[12,32,512]{2,1,0:T(8,128)(2,1)S(1)} %collective-permute-done.10, f16[12,32,512]{2,1,0:T(8,128)(2,1)S(1)} %collective-permute-done.9, f16[12,32,512]{2,1,0:T(8,128)(2,1)S(1)} %collective-permute-done.8, bf16[4,12,32,512]{3,2,1,0:T(8,128)(2,1)S(1)} %collective-permute-done.2, s32[]{:T(128)S(6)} %select_n.93, ...), kind=kLoop, calls=%fused_computation.3 | loop fusion | flops 1966080 | bytes 2752524 | tf_op jit(solution)/shard_map/add | solution.py:219
  44.8 0.6 shard_map.37
  45.4 31.9 %all_to_all.10.pieces_ref = bf16[16,2,32,512]{3,2,1,0:T(8,128)(2,1)S(1)} all-to-all(bf16[16,2,32,512]{3,2,1,0:T(8,128)(2,1)S(1)} %bitcast.64), channel_id=1, replica_groups=mesh['dp'=16,'grp'=16] {'grp'}, dimensions={0} | all-to-all | bytes 2097152 | tf_op jit(solution)/shard_map/all_to_all | solution.py:240
  77.3 10.1 %shard_map.38 = bf16[16,2,32,512]{3,2,1,0:T(8,128)(2,1)S(1)} custom-call(bf16[16,2,32,512]{3,2,1,0:T(8,128)(2,1)S(1)} %all_to_all.10.pieces_ref, f32[2,2,512,512]{3,2,1,0:T(8,128)} %bitcast.75), custom_call_target="tpu_custom_call" | custom-call | tf_op jit(solution)/shard_map/pallas_call | solution.py:89
  87.4 28.7 %all_to_all.11 = bf16[16,2,32,512]{3,2,1,0:T(8,128)(2,1)S(1)} all-to-all(bf16[16,2,32,512]{3,2,1,0:T(8,128)(2,1)S(1)} %shard_map.38), channel_id=1, replica_groups=mesh['dp'=16,'grp'=16] {'grp'}, dimensions={0} | all-to-all | bytes 2097152 | tf_op jit(solution)/shard_map/all_to_all | solution.py:242
  116.1 2.1 %shard_map.39 = f32[12,32,512]{2,1,0:T(8,128)} custom-call(s32[12]{0:T(128)S(1)} %multiply_add_fusion.index_ref, bf16[32,32,512]{2,1,0:T(8,128)(2,1)S(1)} %bitcast.65), custom_call_target="tpu_custom_call" | custom-call | tf_op jit(solution)/shard_map/pallas_call | solution.py:139
  (20 shorter events, 1.9 us)
Async XLA Ops:
  0.0 19.1 %copy-start = (s32[1,12,1]{1,2,0:T(1,128)S(1)}, s32[1,12,1]{1,2,0:T(1,128)}, u32[]{:S(2)}) copy-start(s32[1,12,1]{1,2,0:T(1,128)} %param.4) | copy-start | bytes 148
  1.2 4.7 %collective-permute-start = (bf16[1,12,32,512]{3,2,1,0:T(8,128)(2,1)S(1)}, bf16[1,12,32,512]{3,2,1,0:T(8,128)(2,1)S(1)}, u32[]{:S(2)}, u32[]{:S(2)}) collective-permute-start(bf16[1,12,32,512]{3,2,1,0:T(8,128)(2,1)S(1)} %get-tuple-element.24), channel_id=1, source_target_pairs={{0,16},{16,0},{32,48},{48,32},{64,80},{80,64},{96,112},{112,96},{1... | collective-permute-start | bytes 1179656 | tf_op jit(solution)/shard_map/ppermute | solution.py:158
  4.5 1.9 %collective-permute-start.1 = (bf16[1,12,32,512]{3,2,1,0:T(8,128)(2,1)S(1)}, bf16[1,12,32,512]{3,2,1,0:T(8,128)(2,1)S(1)}, u32[]{:S(2)}, u32[]{:S(2)}) collective-permute-start(bf16[1,12,32,512]{3,2,1,0:T(8,128)(2,1)S(1)} %get-tuple-element.23), channel_id=1, source_target_pairs={{0,16},{16,0},{32,48},{48,32},{64,80},{80,64},{96,112},{112,96},{1... | collective-permute-start | bytes 1179656 | tf_op jit(solution)/shard_map/ppermute | solution.py:158
  9.4 3.5 %collective-permute-start.2 = (bf16[4,12,32,512]{3,2,1,0:T(8,128)(2,1)S(1)}, bf16[4,12,32,512]{3,2,1,0:T(8,128)(2,1)S(1)}, u32[]{:S(2)}, u32[]{:S(2)}) collective-permute-start(bf16[4,12,32,512]{3,2,1,0:T(8,128)(2,1)S(1)} %dynamic-slice_bitcast_fusion), channel_id=1, source_target_pairs={{0,16},{16,0},{32,48},{48,32},{64,80},{80,64},{96,112},{112,96},{1... | collective-permute-start | bytes 4718600 | tf_op jit(solution)/shard_map/ppermute | solution.py:158
  9.8 4.2 %collective-permute-start.3 = (bf16[1,12,32,512]{3,2,1,0:T(8,128)(2,1)S(1)}, bf16[1,12,32,512]{3,2,1,0:T(8,128)(2,1)S(1)}, u32[]{:S(2)}, u32[]{:S(2)}) collective-permute-start(bf16[1,12,32,512]{3,2,1,0:T(8,128)(2,1)S(1)} %get-tuple-element.22), channel_id=1, source_target_pairs={{0,16},{16,0},{32,48},{48,32},{64,80},{80,64},{96,112},{112,96},{1... | collective-permute-start | bytes 1179656 | tf_op jit(solution)/shard_map/ppermute | solution.py:158
  10.0 7.8 %collective-permute-start.4 = (f16[12,32,512]{2,1,0:T(8,128)(2,1)S(1)}, f16[12,32,512]{2,1,0:T(8,128)(2,1)S(1)}, u32[]{:S(2)}, u32[]{:S(2)}) collective-permute-start(f16[12,32,512]{2,1,0:T(8,128)(2,1)S(1)} %get-tuple-element.20), channel_id=1, source_target_pairs={{0,64},{16,208},{32,96},{48,240},{64,0},{80,144},{96,32},{112,176}... | collective-permute-start | bytes 1179656 | tf_op jit(solution)/shard_map/ppermute | solution.py:158
  11.0 12.1 %collective-permute-start.5 = (bf16[1,12,32,512]{3,2,1,0:T(8,128)(2,1)S(1)}, bf16[1,12,32,512]{3,2,1,0:T(8,128)(2,1)S(1)}, u32[]{:S(2)}, u32[]{:S(2)}) collective-permute-start(bf16[1,12,32,512]{3,2,1,0:T(8,128)(2,1)S(1)} %get-tuple-element.21), channel_id=1, source_target_pairs={{0,16},{16,0},{32,48},{48,32},{64,80},{80,64},{96,112},{112,96},{1... | collective-permute-start | bytes 1179656 | tf_op jit(solution)/shard_map/ppermute | solution.py:158
  11.0 13.9 %collective-permute-start.6 = (f16[12,32,512]{2,1,0:T(8,128)(2,1)S(1)}, f16[12,32,512]{2,1,0:T(8,128)(2,1)S(1)}, u32[]{:S(2)}, u32[]{:S(2)}) collective-permute-start(f16[12,32,512]{2,1,0:T(8,128)(2,1)S(1)} %get-tuple-element.19), channel_id=1, source_target_pairs={{0,64},{16,208},{32,96},{48,240},{64,0},{80,144},{96,32},{112,176}... | collective-permute-start | bytes 1179656 | tf_op jit(solution)/shard_map/ppermute | solution.py:158
  19.0 8.3 %collective-permute-start.7 = (f16[12,32,512]{2,1,0:T(8,128)(2,1)S(1)}, f16[12,32,512]{2,1,0:T(8,128)(2,1)S(1)}, u32[]{:S(2)}, u32[]{:S(2)}) collective-permute-start(f16[12,32,512]{2,1,0:T(8,128)(2,1)S(1)} %fusion.11), channel_id=1, source_target_pairs={{0,192},{16,80},{32,224},{48,112},{64,128},{80,16},{96,160},{112,4... | collective-permute-start | bytes 1179656 | tf_op jit(solution)/shard_map/ppermute | solution.py:158
  19.3 24.0 %collective-permute-start.8 = (f16[12,32,512]{2,1,0:T(8,128)(2,1)S(1)}, f16[12,32,512]{2,1,0:T(8,128)(2,1)S(1)}, u32[]{:S(2)}, u32[]{:S(2)}) collective-permute-start(f16[12,32,512]{2,1,0:T(8,128)(2,1)S(1)} %fusion.13), channel_id=1, source_target_pairs={{0,128},{16,144},{32,160},{48,176},{64,192},{80,208},{96,224},{112... | collective-permute-start | bytes 1179656 | tf_op jit(solution)/shard_map/ppermute | solution.py:158
  22.9 20.1 %collective-permute-start.10 = (f16[12,32,512]{2,1,0:T(8,128)(2,1)S(1)}, f16[12,32,512]{2,1,0:T(8,128)(2,1)S(1)}, u32[]{:S(2)}, u32[]{:S(2)}) collective-permute-start(f16[12,32,512]{2,1,0:T(8,128)(2,1)S(1)} %get-tuple-element.18), channel_id=1, source_target_pairs={{0,192},{16,80},{32,224},{48,112},{64,128},{80,16},{96,160},{112,4... | collective-permute-start | bytes 1179656 | tf_op jit(solution)/shard_map/ppermute | solution.py:158
  23.1 20.2 %collective-permute-start.9 = (f16[12,32,512]{2,1,0:T(8,128)(2,1)S(1)}, f16[12,32,512]{2,1,0:T(8,128)(2,1)S(1)}, u32[]{:S(2)}, u32[]{:S(2)}) collective-permute-start(f16[12,32,512]{2,1,0:T(8,128)(2,1)S(1)} %get-tuple-element.17), channel_id=1, source_target_pairs={{0,64},{16,208},{32,96},{48,240},{64,0},{80,144},{96,32},{112,176}... | collective-permute-start | bytes 1179656 | tf_op jit(solution)/shard_map/ppermute | solution.py:158
  28.6 16.0 %collective-permute-start.11 = (f16[12,32,512]{2,1,0:T(8,128)(2,1)S(1)}, f16[12,32,512]{2,1,0:T(8,128)(2,1)S(1)}, u32[]{:S(2)}, u32[]{:S(2)}) collective-permute-start(f16[12,32,512]{2,1,0:T(8,128)(2,1)S(1)} %fusion.4), channel_id=1, source_target_pairs={{0,32},{16,48},{32,0},{48,16},{64,96},{80,112},{96,64},{112,80},{1... | collective-permute-start | bytes 1179656 | tf_op jit(solution)/shard_map/ppermute | solution.py:158
